TPU v7x, 32 devices: a whole 2x2x4 slice. The times are simulated.
32 devices in a mesh: dp: 4 (over y, x), erow: 2 (over core), ecol: 4 (over z).
Axes of the slice: x: 2, y: 2, z: 4, core: 2. Of those that a mesh axis runs over, the one named last changes fastest.
Arguments:
- tokens: bfloat16 [16, 512, 1024], P(('dp', 'ecol'), 'erow'), may hold values from -6 to 6
- lengths: int32 [16], P(('dp', 'ecol')), may hold values from 384 to 512, as said below
- routes: int32 [16, 512, 2], P(('dp', 'ecol'), 'erow'), may hold values from 0 to 7, as said below
- attn_gain: float32 [1024], replicated, may hold values from 0.1 to 1.9
- query_weight: bfloat16 [1024, 1024], replicated, may hold values from -0.1875 to 0.1875
- key_weight: bfloat16 [1024, 1024], replicated, may hold values from -0.1875 to 0.1875
- value_weight: bfloat16 [1024, 1024], replicated, may hold values from -0.1875 to 0.1875
- out_weight: bfloat16 [1024, 1024], replicated, may hold values from -1.5 to 1.5
- relative_bias: float32 [16, 32], replicated, may hold values from -4 to 4
- moe_gain: float32 [1024], replicated, may hold values from 0.1 to 1.9
- router_weight: float32 [1024, 8], replicated, may hold values from -0.09375 to 0.09375
- gate_weight: bfloat16 [8, 1024, 2816], P(('erow', 'ecol')), may hold values from -0.1875 to 0.1875
- up_weight: bfloat16 [8, 1024, 2816], P(('erow', 'ecol')), may hold values from -0.1875 to 0.1875
- down_weight: bfloat16 [8, 2816, 1024], P(('erow', 'ecol')), may hold values from -4 to 4
- cotangent: bfloat16 [16, 512, 1024], P(('dp', 'ecol'), 'erow'), may hold values from -6 to 6
Outputs:
- output: bfloat16 [16, 512, 1024], P(('dp', 'ecol'), 'erow')
- grad_tokens: float32 [16, 512, 1024], P(('dp', 'ecol'), 'erow')
- grad_attn_gain: float32 [1024], P(('dp', 'erow', 'ecol'))
- grad_query: float32 [1024, 1024], P(('dp', 'erow', 'ecol'))
- grad_key: float32 [1024, 1024], P(('dp', 'erow', 'ecol'))
- grad_value: float32 [1024, 1024], P(('dp', 'erow', 'ecol'))
- grad_out: float32 [1024, 1024], P(('dp', 'erow', 'ecol'))
- grad_bias: float32 [512], P(('dp', 'erow', 'ecol'))
- grad_moe_gain: float32 [1024], P(('dp', 'erow', 'ecol'))
- grad_router: float32 [1024, 8], P(('dp', 'erow', 'ecol'))
- grad_gate: float32 [8, 1024, 2816], P(('erow', 'ecol'), 'dp')
- grad_up: float32 [8, 1024, 2816], P(('erow', 'ecol'), 'dp')
- grad_down: float32 [8, 2816, 1024], P(('erow', 'ecol'), 'dp')
Inputs may be any that keep to these rules, and one draw needn't show every extreme that they name: `lengths`: every item has more than 383 live positions; some item has exactly 512. The two experts of a position differ. In every draw one expert is named first at the first 80 positions of every aligned block of 256 positions (the rows of one device); padded positions carry routes too.
All inputs are finite; a program needn't handle non-finite values.
Results may differ from a plain program's by a relative error of at most 0.025.
Values may be sent and summed in bfloat16 or wider, within the bound.
A program may use at most 384 MiB of HBM per device.

v0:
```python
import functools

import jax
import jax.numpy as jnp
from jax import lax
from jax.experimental import pallas as pl
from jax.experimental.pallas import tpu as pltpu
from jax.sharding import PartitionSpec as P

epsilon = 1e-06
highest = lax.Precision.HIGHEST
thresholds = (12, 16, 23, 32, 46, 64, 91)
MESH = pl.DeviceIdType.MESH
LANES = 128
VMEM_LIMIT = 60 * 1024 * 1024


def bucket_of(offset):
    distance = jnp.abs(offset)
    larger = 8 + sum(((distance >= bound_at).astype(jnp.int32) for bound_at in thresholds))
    return jnp.where(offset > 0, 16, 0) + jnp.where(distance < 8, distance, larger)


def product(left_side, right_side):
    return jnp.dot(left_side, right_side, preferred_element_type=jnp.float32)


def product_back(left_side, right_side):
    return lax.dot_general(
        left_side, right_side, (((1,), (1,)), ((), ())), preferred_element_type=jnp.float32
    )


def product_left(left_side, right_side):
    return lax.dot_general(
        left_side, right_side, (((0,), (0,)), ((), ())), preferred_element_type=jnp.float32
    )


def greet(devices):
    barrier = pltpu.get_barrier_semaphore()
    for device in devices:
        pl.semaphore_signal(barrier, 1, device_id=device, device_id_type=MESH)
    pl.semaphore_wait(barrier, len(devices))


def remote(source, target, send_sem, recv_sem, device):
    return pltpu.make_async_remote_copy(
        src_ref=source,
        dst_ref=target,
        send_sem=send_sem,
        recv_sem=recv_sem,
        device_id=device,
        device_id_type=MESH,
    )


def flipped(index, mask, size):
    bit = 1
    while bit < size:
        if mask & bit:
            index = index + bit * (1 - 2 * lax.rem(lax.div(index, bit), 2))
        bit *= 2
    return index


def partners(n_row, n_col):
    row, col = lax.axis_index("erow"), lax.axis_index("ecol")
    return [
        {"erow": flipped(row, place % n_row, n_row), "ecol": flipped(col, place // n_row, n_col)}
        for place in range(n_row * n_col)
    ]


class Spread:
    def __init__(self, near, far, send_sems, recv_sems):
        dp = lax.axis_index("dp")
        slow, fast = lax.div(dp, 2), lax.rem(dp, 2)
        self.devices = [{"dp": slow * 2 + 1 - fast}, {"dp": (1 - slow) * 2 + fast}]
        self.near, self.far, self.send_sems, self.recv_sems = near, far, send_sems, recv_sems

    def first(self, source):
        return [
            remote(source, self.near.at[k], self.send_sems.at[k], self.recv_sems.at[k], self.devices[k])
            for k in range(2)
        ]

    def second(self, near=None):
        near = self.near if near is None else near
        half = self.far.shape[0] // 2
        return [
            remote(
                near.at[k, pl.ds(k * half, half)],
                self.far.at[pl.ds(k * half, half)],
                self.send_sems.at[2 + k],
                self.recv_sems.at[2 + k],
                self.devices[1 - k],
            )
            for k in range(2)
        ]


def start_all(copies):
    for copy in copies:
        copy.start()


def wait_all(copies):
    for copy in copies:
        copy.wait()


class ShareSum:
    stages = 5

    def __init__(self, sizes, depth, grads, totals, held, send_sems, recv_sems):
        self.n_row, self.n_col = sizes
        self.depth, self.grads, self.totals, self.held = depth, grads, totals, held
        self.send_sems, self.recv_sems = send_sems, recv_sems
        dp, self.row, self.col = (lax.axis_index(name) for name in ("dp", "erow", "ecol"))
        self.slow, self.fast = lax.div(dp, 2), lax.rem(dp, 2)
        self.over_row = {"erow": 1 - self.row}
        self.over_fast = {"dp": self.slow * 2 + 1 - self.fast}
        self.over_slow = {"dp": (1 - self.slow) * 2 + self.fast}
        self.over_col = [{"ecol": flipped(self.col, mask, self.n_col)} for mask in range(1, self.n_col)]
        self.devices = [self.over_row, self.over_fast, self.over_slow] + self.over_col

    def parts(self, at):
        width = self.grads[at].shape[-1]
        if width >= 2 * LANES:
            return ((0, pl.ds(0, width // 2)), (1, pl.ds(width // 2, width // 2)))
        return ((0, pl.ds(0, width)),)

    def copy(self, at, number):
        from_row, from_near, from_far, late_sum, from_col = self.held[at]
        sems = (self.send_sems.at[at, number], self.recv_sems.at[at, number])
        if number == 0:
            return remote(self.grads[at].at[:, :, 1 - self.row], from_row, *sems, self.over_row)
        if number <= 4:
            which, cut = self.parts(at)[(number - 1) % 2]
            if number == 1:
                return remote(from_row.at[:, 1 - self.fast, :, cut], from_near.at[:, :, cut], *sems, self.over_fast)
            if number == 2:
                return remote(from_row.at[1 - self.slow, :, :, cut], from_near.at[:, :, cut], *sems, self.over_slow)
            if number == 3:
                return remote(from_near.at[1 - self.slow, :, cut], from_far.at[:, cut], *sems, self.over_slow)
            return remote(from_near.at[1 - self.fast, :, cut], from_far.at[:, cut], *sems, self.over_fast)
        mask = number - 4
        peer = flipped(self.col, mask, self.n_col)
        return remote(late_sum.at[peer], from_col.at[mask - 1], *sems, self.over_col[mask - 1])

    def step(self, at, stage):
        from_row, from_near, from_far, late_sum, from_col = self.held[at]
        if stage == 0:
            self.copy(at, 0).start()
        elif stage == 1:
            self.copy(at, 0).wait()
            for high in range(2):
                for low in range(2):
                    from_row[high, low] = (
                        self.grads[at][high, low, self.row].astype(jnp.float32)
                        + from_row[high, low].astype(jnp.float32)
                    ).astype(from_row.dtype)
            for which, _ in self.parts(at):
                self.copy(at, 1 + which).start()
        elif stage == 2:
            for which, cut in self.parts(at):
                self.copy(at, 1 + which).wait()
                for place in range(2):
                    kept = from_row[place, self.fast, :, cut] if which == 0 else from_row[self.slow, place, :, cut]
                    from_near[place, :, cut] = (
                        kept.astype(jnp.float32) + from_near[place, :, cut].astype(jnp.float32)
                    ).astype(from_near.dtype)
                self.copy(at, 3 + which).start()
        elif stage == 3:
            for which, cut in self.parts(at):
                self.copy(at, 3 + which).wait()
                kept = from_near[self.slow if which == 0 else self.fast, :, cut]
                total = kept.astype(jnp.float32) + from_far[:, cut].astype(jnp.float32)
                late_sum[:, :, cut] = total.reshape(self.n_col, self.depth, -1).astype(late_sum.dtype)
            for mask in range(1, self.n_col):
                self.copy(at, 4 + mask).start()
        else:
            total = late_sum[self.col].astype(jnp.float32)
            for mask in range(1, self.n_col):
                self.copy(at, 4 + mask).wait()
                total = total + from_col[mask - 1].astype(jnp.float32)
            self.totals[at][...] = total

    def turn(self, number):
        for at in range(len(self.grads)):
            if 0 <= number - at < self.stages:
                self.step(at, number - at)

    @property
    def turns(self):
        return len(self.grads) + self.stages - 1


def share_scratch(sizes, depth, width, kind):
    n_row, n_col = sizes
    strip = n_col * depth
    late = kind if depth % 16 == 0 else jnp.float32
    return [
        pltpu.VMEM((2, 2, strip, width), kind),
        pltpu.VMEM((2, strip, width), kind),
        pltpu.VMEM((strip, width), kind),
        pltpu.VMEM((n_col, depth, width), late),
        pltpu.VMEM((n_col - 1, depth, width), late),
    ]


def iota(shape, dimension):
    return lax.broadcasted_iota(jnp.int32, shape, dimension)


def row_slots(routes, live, experts, room, capacity):
    tok = live.shape[1]
    names = iota((experts, tok), 0)
    hot = [(routes[k : k + 1] == names) & live for k in range(2)]
    both = jnp.where(hot[0] | hot[1], 1.0, 0.0).astype(jnp.bfloat16)
    before = jnp.where(iota((tok, tok), 0) < iota((tok, tok), 1), 1.0, 0.0).astype(jnp.bfloat16)
    earlier = product(both, before)
    slots = []
    for k in range(2):
        place = jnp.sum(jnp.where(hot[k], earlier, 0.0), axis=0, keepdims=True)
        slot = routes[k : k + 1].astype(jnp.float32) * room + place
        slots.append(jnp.where(live & (place < capacity), slot, -1.0))
    return slots


def bias_tables(relative_bias, table_width, offset):
    buckets = relative_bias.shape[1]
    place = iota((buckets, table_width), 1)
    distance = jnp.where(place < table_width // 2, place, place - table_width) + offset
    hot = jnp.where(bucket_of(distance) == iota((buckets, table_width), 0), 1.0, 0.0)
    return jnp.dot(relative_bias, hot, precision=highest, preferred_element_type=jnp.float32)


def skewed(row, rows):
    width = row.shape[1]
    full = pltpu.roll(jnp.broadcast_to(row, (rows, width)), 0, 1, stride=1, stride_axis=0)
    return full[:, : width // 2]


def front_kernel(
    dims,
    lengths,
    tokens,
    cotangent,
    routes_row,
    routes_col,
    attn_gain,
    moe_gain,
    relative_bias,
    router,
    query_weight,
    key_weight,
    value_weight,
    out_weight,
    normed_out,
    query_out,
    both_out,
    probs_out,
    mixed_out,
    residual_out,
    gates_out,
    rows_out,
    cot_landed,
    cot_near,
    select,
    cot_slots,
    tables,
    held_weights,
    weight_sems,
    own_sem,
    send_sems,
    recv_sems,
    row_send,
    row_recv,
    near_send,
    near_recv,
):
    heads, experts, room, capacity, n_row, n_col = dims
    tok, width = tokens.shape
    pair_width = 2 * width // heads
    loads = []
    for at, source in enumerate((key_weight, value_weight, query_weight, out_weight)):
        load = pltpu.make_async_copy(source, held_weights.at[at], weight_sems.at[at])
        load.start()
        loads.append(load)
    devices = partners(n_row, n_col)
    spread = Spread(cot_near, None, near_send, near_recv)
    part = len(devices) // 2
    barrier = pltpu.get_barrier_semaphore()
    for device in devices[1:] + spread.devices:
        pl.semaphore_signal(barrier, 1, device_id=device, device_id_type=MESH)

    piece = lax.axis_index("erow")
    length = lengths[0]
    live = iota((1, tok), 1) + piece * tok < length
    slots = row_slots(routes_row[...], live, experts, room, capacity)
    names = iota((experts * room, tok), 0).astype(jnp.float32)
    hot = [jnp.where(names == slot, 1.0, 0.0).astype(jnp.bfloat16) for slot in slots]
    select[...] = hot[0] + hot[1]
    cot_slots[...] = product(select[...], cotangent[...]).astype(jnp.bfloat16).reshape(cot_slots.shape)
    pl.semaphore_wait(barrier, len(devices) + 1)
    own = pltpu.make_async_copy(cot_slots.at[0], cot_landed.at[0], own_sem)
    own.start()
    copies = []
    for place in range(1, len(devices)):
        copy = remote(
            cot_slots.at[place],
            cot_landed.at[place],
            send_sems.at[place - 1],
            recv_sems.at[place - 1],
            devices[place],
        )
        copy.start()
        copies.append(copy)

    inputs = tokens[...].astype(jnp.float32)
    scale = lax.rsqrt(jnp.mean(inputs * inputs, axis=1, keepdims=True) + epsilon)
    normed = (inputs * scale * attn_gain[...]).astype(jnp.bfloat16)
    normed_out[...] = normed
    loads[0].wait()
    both_out[:tok, :width] = product(normed, held_weights[0]).astype(jnp.bfloat16)
    loads[1].wait()
    both_out[:tok, width:] = product(normed, held_weights[1]).astype(jnp.bfloat16)
    pair_copy = remote(both_out.at[pl.ds(0, tok)], both_out.at[pl.ds(tok, tok)], row_send, row_recv, devices[1])
    pair_copy.start()
    loads[2].wait()
    query_out[...] = (product(normed, held_weights[2]) * 0.125).astype(jnp.bfloat16)
    offset = tok * (1 - 2 * piece)
    tables[:, : 2 * tok] = bias_tables(relative_bias[...], 2 * tok, 0)
    tables[:, 2 * tok :] = bias_tables(relative_bias[...], 2 * tok, offset)
    place = iota((1, 2 * tok), 1)
    position = jnp.where(place < tok, place + piece * tok, place - tok + (1 - piece) * tok)
    dead = jnp.where(position < length, 0.0, -1000000000.0)
    low_half = iota((tok, pair_width), 1) < pair_width // 2
    pair_copy.wait()

    def attend(pair, carry):
        lanes = pl.ds(pl.multiple_of(pair * pair_width, pair_width), pair_width)
        value_lanes = pl.ds(pl.multiple_of(width + pair * pair_width, pair_width), pair_width)
        queries, keys, values = query_out[:, lanes], both_out[:, lanes], both_out[:, value_lanes]

        @pl.when(pair == 1)
        def _():
            wait_all([own] + copies[: part - 1])
            start_all(spread.first(cot_landed.at[pl.ds(0, part)]))

        results = []
        for member in range(2):
            mask = low_half if member == 0 else jnp.logical_not(low_half)
            head = 2 * pair + member
            scores = product_back(jnp.where(mask, queries, jnp.zeros_like(queries)), keys)
            table = tables[pl.ds(head, 1)]
            bias = jnp.concatenate([skewed(table[:, : 2 * tok], tok), skewed(table[:, 2 * tok :], tok)], axis=1)
            scores = scores + bias + dead
            powers = jnp.exp(scores - jnp.max(scores, axis=1, keepdims=True))
            probs = (powers * (1.0 / jnp.sum(powers, axis=1, keepdims=True))).astype(jnp.bfloat16)
            probs_out[pl.ds(head, 1)] = probs[None]
            results.append(product(probs, values))
        mixed_out[:, lanes] = jnp.where(low_half, results[0], results[1]).astype(jnp.bfloat16)
        return carry

    lax.fori_loop(0, heads // 2, attend, 0)
    loads[3].wait()
    residual = inputs + product(mixed_out[...], held_weights[3])
    residual_out[...] = residual
    scale = lax.rsqrt(jnp.mean(residual * residual, axis=1, keepdims=True) + epsilon)
    moe_in = residual * scale * moe_gain[...]
    logits = jnp.dot(moe_in, router[...], precision=highest, preferred_element_type=jnp.float32)
    lane = iota(logits.shape, 1)
    logits = jnp.where(lane < experts, logits, -1e30)
    powers = jnp.exp(logits - jnp.max(logits, axis=1, keepdims=True))
    gates = powers / jnp.sum(powers, axis=1, keepdims=True)
    gates_out[...] = gates
    panel = jnp.zeros((experts * room, LANES), jnp.float32)
    for k in range(2):
        pick = jnp.sum(jnp.where(routes_col[:, k : k + 1] == lane, gates, 0.0), axis=1, keepdims=True)
        high = pick.astype(jnp.bfloat16)
        low = (pick - high.astype(jnp.float32)).astype(jnp.bfloat16)
        parts = jnp.where(lane == 0, high, jnp.where(lane == 1, low, jnp.zeros_like(low)))
        panel = panel + product(hot[k], parts)
    rows = product(select[...], moe_in.astype(jnp.bfloat16))
    rows_out[:, :, :width] = rows.astype(jnp.bfloat16).reshape(rows_out.shape[0], -1, width)
    rows_out[:, :, width:] = panel.astype(jnp.bfloat16).reshape(rows_out.shape[0], -1, LANES)
    wait_all(copies[part - 1 :])
    wait_all(spread.first(cot_landed.at[pl.ds(0, part)]))


def front(dims, number, lengths, tokens, cotangent, routes_row, routes_col, *params):
    heads, experts, room, capacity, n_row, n_col = dims
    tok, width = tokens.shape
    group = n_row * n_col
    blocks = experts * room // group
    half, single = jnp.bfloat16, jnp.float32
    vmem, anywhere = pl.BlockSpec(memory_space=pltpu.VMEM), pl.BlockSpec(memory_space=pl.ANY)
    shapes = [
        ((tok, width), half),
        ((tok, width), half),
        ((2 * tok, 2 * width), half),
        ((heads, tok, 2 * tok), half),
        ((tok, width), half),
        ((tok, width), single),
        ((tok, LANES), single),
        ((group, blocks, width + LANES), half),
        ((group, blocks, width), half),
        ((2, group // 2, blocks, width), half),
    ]
    return pl.pallas_call(
        functools.partial(front_kernel, dims),
        out_shape=[jax.ShapeDtypeStruct(shape, kind) for shape, kind in shapes],
        in_specs=[pl.BlockSpec(memory_space=pltpu.SMEM)] + [vmem] * 8 + [anywhere] * 4,
        out_specs=[vmem] * 8 + [anywhere] * 2,
        scratch_shapes=[
            pltpu.VMEM((experts * room, tok), half),
            pltpu.VMEM((group, blocks, width), half),
            pltpu.VMEM((heads, 4 * tok), single),
            pltpu.VMEM((4, width, width), half),
            pltpu.SemaphoreType.DMA((4,)),
            pltpu.SemaphoreType.DMA,
            pltpu.SemaphoreType.DMA((group - 1,)),
            pltpu.SemaphoreType.DMA((group - 1,)),
            pltpu.SemaphoreType.DMA,
            pltpu.SemaphoreType.DMA,
            pltpu.SemaphoreType.DMA((2,)),
            pltpu.SemaphoreType.DMA((2,)),
        ],
        compiler_params=pltpu.CompilerParams(
            collective_id=number, has_side_effects=True, vmem_limit_bytes=VMEM_LIMIT
        ),
    )(lengths, tokens, cotangent, routes_row, routes_col, *params)


def expert_kernel(
    tile,
    sizes,
    rows_sent,
    cot_own,
    cot_near,
    gate_weight,
    up_weight,
    down_weight,
    back_landed,
    rows_landed,
    out_rows,
    hidden_all,
    gate_back_all,
    up_back_all,
    cot_far,
    cot_near_late,
    cot_far_late,
    rows_near,
    rows_far,
    gate_mat,
    up_mat,
    down_mat,
    cot,
    down_rows,
    total,
    picks_back,
    back_sent,
    load_sems,
    own_sems,
    send_sems,
    recv_sems,
    spread_send,
    spread_recv,
):
    group, room, width = cot_own.shape
    hidden_width = gate_mat.shape[1]
    loads = []
    for at, (source, target) in enumerate(
        ((cot_own, cot), (down_weight, down_mat), (gate_weight, gate_mat), (up_weight, up_mat))
    ):
        load = pltpu.make_async_copy(source, target, load_sems.at[at])
        load.start()
        loads.append(load)
    devices = partners(*sizes)
    part = group // 2
    spreads = [
        Spread(near, far, spread_send.at[at], spread_recv.at[at])
        for at, (near, far) in enumerate(((cot_near, cot_far), (cot_near_late, cot_far_late), (rows_near, rows_far)))
    ]
    late_cots = cot_own.at[pl.ds(part, part)]
    early_rows = rows_landed.at[pl.ds(0, part)]
    greet(devices[1:] + spreads[0].devices)
    copies = {}
    for place in range(group):
        if place == 0:
            copy = pltpu.make_async_copy(rows_sent.at[0], rows_landed.at[0], own_sems.at[0])
        else:
            copy = remote(
                rows_sent.at[place],
                rows_landed.at[place],
                send_sems.at[0, place - 1],
                recv_sems.at[0, place - 1],
                devices[place],
            )
        copy.start()
        copies[0, place] = copy
    start_all(spreads[0].second())
    start_all(spreads[1].first(late_cots))
    tiles = hidden_width // tile
    loads[0].wait()
    loads[1].wait()
    cot_rows = cot[...].reshape(group * room, width)

    def early(at, carry):
        cut = pl.ds(pl.multiple_of(at * tile, tile), tile)
        down_rows[:, cut] = product_back(cot_rows, down_mat[cut, :]).astype(jnp.bfloat16)
        return carry

    lax.fori_loop(0, tiles, early, 0)
    loads[2].wait()
    loads[3].wait()
    for half in range(2):
        places = range(half * part, (half + 1) * part)
        for place in places:
            copies[0, place].wait()
        if half == 0:
            start_all(spreads[2].first(early_rows))
        held = slice(half * part, (half + 1) * part)
        strip = slice(half * part * room, (half + 1) * part * room)
        rows = rows_landed[held, :, :width].reshape(part * room, width)
        panel = rows_landed[held, :, width:].reshape(part * room, LANES)
        picks = panel[:, 0:1].astype(jnp.float32) + panel[:, 1:2].astype(jnp.float32)
        total[...] = jnp.zeros_like(total)
        picks_back[...] = jnp.zeros_like(picks_back)

        def middle(at, carry):
            cut = pl.ds(pl.multiple_of(at * tile, tile), tile)
            value, slope = gelu_parts(product(rows, gate_mat[:, cut]))
            up_part = product(rows, up_mat[:, cut])
            hidden = value * up_part
            hidden_all[strip, cut] = hidden.astype(jnp.bfloat16)
            back = down_rows[strip, cut].astype(jnp.float32)
            weighed = hidden * back
            picks_back[...] += sum(weighed[:, at : at + LANES] for at in range(0, tile, LANES))
            back = back * picks
            gate_back = (back * up_part * slope).astype(jnp.bfloat16)
            up_back = (back * value).astype(jnp.bfloat16)
            gate_back_all[strip, cut] = gate_back
            up_back_all[strip, cut] = up_back
            total[...] += product_back(gate_back, gate_mat[:, cut]) + product_back(up_back, up_mat[:, cut])
            return carry

        lax.fori_loop(0, tiles, middle, 0)
        back_sent[held, :, :width] = total[...].astype(jnp.bfloat16).reshape(part, room, width)
        pick = jnp.sum(picks_back[...], axis=1, keepdims=True)
        high = pick.astype(jnp.bfloat16)
        low = (pick - high.astype(jnp.float32)).astype(jnp.bfloat16)
        lane = iota((part * room, LANES), 1)
        parts = jnp.where(lane == 0, high, jnp.where(lane == 1, low, jnp.zeros_like(low)))
        back_sent[held, :, width:] = parts.reshape(part, room, LANES)
        for place in places:
            if place == 0:
                copy = pltpu.make_async_copy(back_sent.at[0], back_landed.at[0], own_sems.at[1])
            else:
                copy = remote(
                    back_sent.at[place],
                    back_landed.at[place],
                    send_sems.at[1, place - 1],
                    recv_sems.at[1, place - 1],
                    devices[place],
                )
            copy.start()
            copies[1, place] = copy
        if half == 0:
            wait_all(spreads[1].first(late_cots))
            start_all(spreads[1].second())
        else:
            wait_all(spreads[2].first(early_rows))
            start_all(spreads[2].second())

    def outward(at, carry):
        cut = pl.ds(pl.multiple_of(at * tile, tile), tile)
        out = product(hidden_all[...], down_mat[:, cut]).astype(jnp.bfloat16)
        out_rows[:, :, cut] = out.reshape(group, room, tile)
        return carry

    lax.fori_loop(0, width // tile, outward, 0)
    for place in range(group):
        copies[1, place].wait()
    for spread in spreads:
        wait_all(spread.second())


def experts_apply(sizes, number, rows_sent, cot_own, cot_near, gate_weight, up_weight, down_weight):
    group, room, width = cot_own.shape
    hidden_width = gate_weight.shape[1]
    slots = group * room
    half, single = jnp.bfloat16, jnp.float32
    vmem, anywhere = pl.BlockSpec(memory_space=pltpu.VMEM), pl.BlockSpec(memory_space=pl.ANY)
    shapes = [
        rows_sent.shape,
        rows_sent.shape,
        cot_own.shape,
        (slots, hidden_width),
        (slots, hidden_width),
        (slots, hidden_width),
        (group // 2, room, width),
        (2, group // 2, room, width),
        (group // 2, room, width),
        (2, group // 2, room, rows_sent.shape[2]),
        (group // 2, room, rows_sent.shape[2]),
    ]
    return pl.pallas_call(
        functools.partial(expert_kernel, 256, sizes),
        out_shape=[jax.ShapeDtypeStruct(shape, half) for shape in shapes],
        in_specs=[anywhere] * 6,
        out_specs=[anywhere] + [vmem] * 5 + [anywhere] * 5,
        scratch_shapes=[
            pltpu.VMEM((width, hidden_width), half),
            pltpu.VMEM((width, hidden_width), half),
            pltpu.VMEM((hidden_width, width), half),
            pltpu.VMEM((group, room, width), half),
            pltpu.VMEM((slots, hidden_width), half),
            pltpu.VMEM((slots // 2, width), single),
            pltpu.VMEM((slots // 2, LANES), single),
            pltpu.VMEM(rows_sent.shape, half),
            pltpu.SemaphoreType.DMA((4,)),
            pltpu.SemaphoreType.DMA((2,)),
            pltpu.SemaphoreType.DMA((2, group - 1)),
            pltpu.SemaphoreType.DMA((2, group - 1)),
            pltpu.SemaphoreType.DMA((3, 4)),
            pltpu.SemaphoreType.DMA((3, 4)),
        ],
        compiler_params=pltpu.CompilerParams(
            collective_id=number, has_side_effects=True, vmem_limit_bytes=VMEM_LIMIT
        ),
    )(rows_sent, cot_own, cot_near, gate_weight, up_weight, down_weight)


def column_slots(routes, live, experts, room, capacity):
    tok = live.shape[0]
    names = iota((tok, experts), 1)
    hot = [(routes[:, k : k + 1] == names) & live for k in range(2)]
    both = jnp.where(hot[0] | hot[1], 1.0, 0.0).astype(jnp.bfloat16)
    before = jnp.where(iota((tok, tok), 1) < iota((tok, tok), 0), 1.0, 0.0).astype(jnp.bfloat16)
    earlier = product(before, both)
    slots = []
    for k in range(2):
        place = jnp.sum(jnp.where(hot[k], earlier, 0.0), axis=1, keepdims=True)
        slot = routes[:, k : k + 1].astype(jnp.float32) * room + place
        slots.append(jnp.where(live & (place < capacity), slot, -1.0))
    return slots


def halves(values):
    high = values.astype(jnp.bfloat16)
    return high, (values - high.astype(jnp.float32)).astype(jnp.bfloat16)


def back_kernel(
    dims,
    lengths,
    tokens,
    cotangent,
    near_col,
    routes_col,
    attn_gain,
    moe_gain,
    router,
    residual_in,
    gates_in,
    mixed,
    probs_in,
    queries_in,
    both,
    back_in,
    out_sent,
    rows_own,
    query_weight,
    key_weight,
    value_weight,
    out_weight,
    output,
    token_grad,
    branch_grad,
    query_grad,
    key_grad,
    value_grad,
    small,
    rows_near,
    rows_far,
    back,
    out_landed,
    held_weights,
    mixed_back,
    residual_grad,
    far_sent,
    far_landed,
    near_sum,
    diagonals,
    load_sems,
    own_sem,
    send_sems,
    recv_sems,
    row_send,
    row_recv,
    near_send,
    near_recv,
):
    heads, experts, room, capacity, n_row, n_col, share, depth = dims
    tok, width = tokens.shape
    pair_width = 2 * width // heads
    member_width = pair_width // 2
    slots_count = experts * room
    loads = []
    for at, (source, target) in enumerate(
        ((back_in, back), (out_weight, held_weights.at[0]))
        + tuple((w, held_weights.at[1 + k]) for k, w in enumerate((query_weight, key_weight, value_weight)))
    ):
        load = pltpu.make_async_copy(source, target, load_sems.at[at])
        load.start()
        loads.append(load)
    devices = partners(n_row, n_col)
    spread = Spread(rows_near, rows_far, near_send, near_recv)
    part = len(devices) // 2
    late_rows = rows_own.at[pl.ds(part, part)]
    greet(devices[1:] + spread.devices)
    start_all(spread.first(late_rows))
    copies = [pltpu.make_async_copy(out_sent.at[0], out_landed.at[0], own_sem)]
    for place in range(1, len(devices)):
        copies.append(
            remote(
                out_sent.at[place],
                out_landed.at[place],
                send_sems.at[place - 1],
                recv_sems.at[place - 1],
                devices[place],
            )
        )
    for copy in copies:
        copy.start()

    piece = lax.axis_index("erow")
    live = iota((tok, 1), 0) + piece * tok < lengths[0]
    slots = column_slots(near_col[...], live, experts, room, capacity)
    names = iota((tok, slots_count), 1).astype(jnp.float32)
    hot = [jnp.where(names == slot, 1.0, 0.0).astype(jnp.bfloat16) for slot in slots]
    lane = iota((tok, LANES), 1)
    chosen = [routes_col[:, k : k + 1] == lane for k in range(2)]
    gates = gates_in[...]

    residual = residual_in[...]
    scale = lax.rsqrt(jnp.mean(residual * residual, axis=1, keepdims=True) + epsilon)
    moe_in = (residual * scale * moe_gain[...]).astype(jnp.bfloat16)
    loads[0].wait()
    panel = back[:, :, width:].reshape(slots_count, LANES)
    prob_back = jnp.zeros((tok, LANES), jnp.float32)
    for k in range(2):
        parts = product(hot[k], panel)
        prob_back = prob_back + jnp.where(chosen[k], parts[:, 0:1] + parts[:, 1:2], 0.0)
    logit_back = gates * (prob_back - jnp.sum(gates * prob_back, axis=1, keepdims=True))
    logit_high, logit_low = halves(logit_back)
    router_high, router_low = halves(router[...])
    moe_back = (
        product(hot[0] + hot[1], back[:, :, :width].reshape(slots_count, width))
        + product_back(logit_high, router_high)
        + product_back(logit_low, router_high)
        + product_back(logit_high, router_low)
    )
    left = moe_in.T
    router_grad = product(left, logit_high) + product(left, logit_low)
    moe_gain_grad = jnp.sum(residual * scale * moe_back, axis=0, keepdims=True)
    pulled = moe_gain[...] * moe_back
    total = (
        cotangent[...].astype(jnp.float32)
        + scale * pulled
        - residual * (scale * scale * scale * jnp.mean(residual * pulled, axis=1, keepdims=True))
    )
    residual_grad[...] = total
    branch = total.astype(jnp.bfloat16)
    branch_grad[...] = branch
    loads[1].wait()
    mixed_back[...] = product_back(branch, held_weights[0]).astype(jnp.bfloat16)
    reversal = jnp.where(iota((tok, tok), 0) + iota((tok, tok), 1) == tok - 1, 1.0, 0.0).astype(jnp.bfloat16)
    low_half = iota((tok, pair_width), 1) < member_width

    def unattend(pair, carry):
        lanes = pl.ds(pl.multiple_of(pair * pair_width, pair_width), pair_width)
        value_lanes = pl.ds(pl.multiple_of(width + pair * pair_width, pair_width), pair_width)
        keys, values = both[:, lanes], both[:, value_lanes]
        grads = mixed_back[:, lanes]

        @pl.when(pair == heads // 2 - 2)
        def _():
            wait_all(spread.first(late_rows))
            start_all(spread.second())

        queries_left, grads_left = queries_in[:, lanes].T, grads.T
        query_parts, key_parts, value_parts = [], [], []
        for member in range(2):
            head = 2 * pair + member
            mask = low_half if member == 0 else jnp.logical_not(low_half)
            low = probs_in[pl.ds(head, 1)][0]
            probs = low.astype(jnp.float32)
            part = product_back(jnp.where(mask, grads, jnp.zeros_like(grads)), values)
            weighed = probs * part
            score = (weighed - probs * jnp.sum(weighed, axis=1, keepdims=True)).astype(jnp.bfloat16)
            query_parts.append(product(score, keys))
            span = slice(member * member_width, (member + 1) * member_width)
            key_parts.append(product(queries_left[span], score))
            value_parts.append(product(grads_left[span], low))
            exact = product(reversal, score)
            empty = jnp.zeros((tok, tok), jnp.float32)
            padded = jnp.concatenate([exact[:, :tok], empty, exact[:, tok:], empty], axis=1)
            turned = pltpu.roll(padded, 3 * tok + 1, 1, stride=1, stride_axis=0)
            diagonals[pl.ds(head, 1)] = jnp.sum(turned, axis=0, keepdims=True)
        query_grad[:, lanes] = (jnp.where(low_half, query_parts[0], query_parts[1]) * 0.125).astype(jnp.bfloat16)
        key_part = jnp.concatenate(key_parts, axis=0).T
        value_part = jnp.concatenate(value_parts, axis=0).T
        near_sum[:, lanes] = key_part[:tok]
        near_sum[:, value_lanes] = value_part[:tok]
        far_sent[:, lanes] = key_part[tok:].astype(jnp.bfloat16)
        far_sent[:, value_lanes] = value_part[tok:].astype(jnp.bfloat16)
        return carry

    lax.fori_loop(0, heads // 2, unattend, 0)
    pair_copy = remote(far_sent, far_landed, row_send, row_recv, devices[1])
    pair_copy.start()

    segment = width // heads
    table = 4 * tok
    entry = iota((table, LANES), 0)
    other = entry >= table // 4
    other = other & (entry < 3 * table // 4)
    distance = jnp.where(
        other,
        entry - table // 2 + tok * (1 - 2 * piece),
        jnp.where(entry < table // 2, entry, entry - table),
    )
    bucket = bucket_of(distance)
    place = depth * lax.div(bucket, share) + lax.rem(bucket, share)
    target = lax.rem(iota((table, LANES), 1), segment)
    sorted_hot = jnp.where(place == target, 1.0, 0.0).astype(jnp.bfloat16)
    diagonal_high, diagonal_low = halves(diagonals[...])
    bias_rows = product(diagonal_high, sorted_hot) + product(diagonal_low, sorted_hot)
    bias_wide = jnp.concatenate([bias_rows] * (width // LANES), axis=1)
    mine = lax.div(iota((heads, width), 1), segment) == iota((heads, width), 0)
    bias_row = jnp.sum(jnp.where(mine, bias_wide, 0.0), axis=0, keepdims=True)

    loads[2].wait()
    normed_back = product_back(query_grad[...], held_weights[1])
    pair_copy.wait()
    key_total = (near_sum[:, :width] + far_landed[:, :width].astype(jnp.float32)).astype(jnp.bfloat16)
    value_total = (near_sum[:, width:] + far_landed[:, width:].astype(jnp.float32)).astype(jnp.bfloat16)
    key_grad[...] = key_total
    value_grad[...] = value_total
    loads[3].wait()
    loads[4].wait()
    normed_back = normed_back + product_back(key_total, held_weights[2]) + product_back(value_total, held_weights[3])
    inputs = tokens[...].astype(jnp.float32)
    scale = lax.rsqrt(jnp.mean(inputs * inputs, axis=1, keepdims=True) + epsilon)
    attn_gain_grad = jnp.sum(inputs * scale * normed_back, axis=0, keepdims=True)
    pulled = attn_gain[...] * normed_back
    token_grad[...] = (
        residual_grad[...]
        + scale * pulled
        - inputs * (scale * scale * scale * jnp.mean(inputs * pulled, axis=1, keepdims=True))
    )
    empty = jnp.zeros((LANES - 3, width), jnp.float32)
    small[...] = jnp.concatenate([empty, attn_gain_grad, moe_gain_grad, bias_row], axis=0).T + router_grad

    for copy in copies:
        copy.wait()
    results = out_landed[...].reshape(slots_count, width)
    total = residual
    for k in range(2):
        pick = jnp.sum(jnp.where(chosen[k], gates, 0.0), axis=1, keepdims=True)
        total = total + pick * product(hot[k], results)
    output[...] = total.astype(jnp.bfloat16)
    wait_all(spread.second())


def backward(dims, number, *operands):
    heads, experts, room, capacity, n_row, n_col, share, depth = dims
    tokens, back_in, out_sent, rows_own = operands[1], operands[14], operands[15], operands[16]
    tok, width = tokens.shape
    group = n_row * n_col
    half, single = jnp.bfloat16, jnp.float32
    vmem, anywhere = pl.BlockSpec(memory_space=pltpu.VMEM), pl.BlockSpec(memory_space=pl.ANY)
    shapes = [((tok, width), half), ((tok, width), single)] + [((tok, width), half)] * 4 + [((width, LANES), single)]
    shapes += [((2, group // 2) + rows_own.shape[1:], half), ((group // 2,) + rows_own.shape[1:], half)]
    return pl.pallas_call(
        functools.partial(back_kernel, dims),
        out_shape=[jax.ShapeDtypeStruct(shape, kind) for shape, kind in shapes],
        in_specs=[pl.BlockSpec(memory_space=pltpu.SMEM)] + [vmem] * 13 + [anywhere] * 7,
        out_specs=[vmem] * 7 + [anywhere] * 2,
        scratch_shapes=[
            pltpu.VMEM(back_in.shape, half),
            pltpu.VMEM(out_sent.shape, half),
            pltpu.VMEM((4, width, width), half),
            pltpu.VMEM((tok, width), half),
            pltpu.VMEM((tok, width), single),
            pltpu.VMEM((tok, 2 * width), half),
            pltpu.VMEM((tok, 2 * width), half),
            pltpu.VMEM((tok, 2 * width), single),
            pltpu.VMEM((heads, 4 * tok), single),
            pltpu.SemaphoreType.DMA((5,)),
            pltpu.SemaphoreType.DMA,
            pltpu.SemaphoreType.DMA((group - 1,)),
            pltpu.SemaphoreType.DMA((group - 1,)),
            pltpu.SemaphoreType.DMA,
            pltpu.SemaphoreType.DMA,
            pltpu.SemaphoreType.DMA((4,)),
            pltpu.SemaphoreType.DMA((4,)),
        ],
        compiler_params=pltpu.CompilerParams(
            collective_id=number, has_side_effects=True, vmem_limit_bytes=VMEM_LIMIT
        ),
    )(*operands)


def last_kernel(tile, sizes, depth, *refs):
    pieces = 5
    (normed, query_grad, key_grad, value_grad, mixed, branch_grad, small), refs = refs[:7], refs[7:]
    rows_in, refs = refs[:pieces], refs[pieces:]
    cots_in, refs = refs[:pieces], refs[pieces:]
    (own_in, weights, sums), refs = (refs[:3], refs[3:6], refs[6:11]), refs[11:]
    (gate_out, up_out, down_out), refs = refs[:3], refs[3:]
    (rows, cots, rows_left, mats, own_tiles, tiles_of, own_mats, out_tiles, down_tiles), refs = refs[:9], refs[9:]
    grads, refs = refs[:4], refs[4:]
    held, refs = [refs[5 * at : 5 * at + 5] for at in range(5)], refs[25:]
    load_sems, weight_sems, own_sems, out_sems, down_sem, send_sems, recv_sems = refs
    width, strip = normed.shape[1], grads[0].shape[3]
    hidden_width = weights[0].shape[1]
    tiles = hidden_width // tile
    slots = own_in[0].shape[0]
    total_rows = rows.shape[0]
    share = width // 4
    hidden_share = hidden_width // 4
    replica = lax.axis_index("dp")
    summed = ShareSum(sizes, depth, list(grads) + [small], sums, held, send_sems, recv_sems)
    barrier = pltpu.get_barrier_semaphore()
    for device in summed.devices:
        pl.semaphore_signal(barrier, 1, device_id=device, device_id_type=MESH)
    loads, start = [], 0
    for at, (row_piece, cot_piece) in enumerate(zip(rows_in, cots_in)):
        size = row_piece.shape[0]
        for number, (piece, target) in enumerate(((row_piece, rows), (cot_piece, cots))):
            load = pltpu.make_async_copy(piece, target.at[pl.ds(start, size)], load_sems.at[number, at])
            load.start()
            loads.append(load)
        start += size

    def weight_loads(at, slot):
        cut = pl.ds(pl.multiple_of(at * tile, tile), tile)
        return [
            pltpu.make_async_copy(source, mats.at[number, slot], weight_sems.at[number, slot])
            for number, source in enumerate((weights[0].at[:, cut], weights[1].at[:, cut]))
        ] + [pltpu.make_async_copy(weights[2].at[cut], own_mats.at[slot], weight_sems.at[2, slot])]

    def own_loads(at, slot):
        cut = pl.ds(pl.multiple_of(at * tile, tile), tile)
        return [
            pltpu.make_async_copy(
                source.at[:, cut], own_tiles.at[number, slot], own_sems.at[number, slot]
            )
            for number, source in enumerate(own_in)
        ]

    def out_copies(at, slot):
        cut = pl.ds(pl.multiple_of(at * tile, tile), tile)
        return [
            pltpu.make_async_copy(out_tiles.at[number, slot], target.at[:, cut], out_sems.at[number, slot])
            for number, target in enumerate((gate_out, up_out))
        ]

    for load in weight_loads(0, 0) + own_loads(0, 0):
        load.start()
    left = mixed[...].T
    shape = grads[0].shape
    grads[0][...] = product(left, branch_grad[...]).astype(jnp.bfloat16).reshape(shape)
    left = normed[...].T
    pl.semaphore_wait(barrier, len(summed.devices))
    summed.turn(0)
    grads[1][...] = product(left, query_grad[...]).astype(jnp.bfloat16).reshape(shape)
    grads[2][...] = product(left, key_grad[...]).astype(jnp.bfloat16).reshape(shape)
    grads[3][...] = product(left, value_grad[...]).astype(jnp.bfloat16).reshape(shape)
    summed.turn(1)
    for load in loads:
        load.wait()

    def weigh(at, carry):
        cut = pl.ds(pl.multiple_of(at * 256, 256), 256)
        panel = rows[cut, width:]
        picks = panel[:, 0:1].astype(jnp.float32) + panel[:, 1:2].astype(jnp.float32)
        cots[cut] = (cots[cut].astype(jnp.float32) * picks).astype(jnp.bfloat16)
        lanes = pl.ds(pl.multiple_of(replica * share, share), share)
        rows_left[:, cut] = rows[cut, lanes].T
        return carry

    lax.fori_loop(0, total_rows // 256, weigh, 0)
    first = lax.div(replica * hidden_share, tile)
    last = lax.div((replica + 1) * hidden_share - 1, tile)

    def each_tile(at, carry):
        slot = lax.rem(at, 2)
        for load in weight_loads(at, slot) + own_loads(at, slot):
            load.wait()

        @pl.when(at + 1 < tiles)
        def _():
            for load in weight_loads(at + 1, 1 - slot) + own_loads(at + 1, 1 - slot):
                load.start()

        for number in range(2, summed.turns):
            @pl.when(at == number - 2)
            def _(number=number):
                summed.turn(number)

        def each_block(block, carry):
            cut = pl.ds(pl.multiple_of(block * slots, slots), slots)
            value, slope = gelu_parts(product(rows[cut, :width], mats[0, slot]))
            up_part = product(rows[cut, :width], mats[1, slot])
            back = product_back(cots[cut], own_mats[slot])
            place = pl.ds(pl.multiple_of((block - 1) * slots, slots), slots)
            tiles_of[0, place] = (value * up_part).astype(jnp.bfloat16)
            tiles_of[1, place] = (back * up_part * slope).astype(jnp.bfloat16)
            tiles_of[2, place] = (back * value).astype(jnp.bfloat16)
            return carry

        lax.fori_loop(1, total_rows // slots, each_block, 0)

        @pl.when(at >= 2)
        def _():
            for copy in out_copies(at - 2, slot):
                copy.wait()

        for number in range(2):
            out_tiles[number, slot] = product(rows_left[:, :slots], own_tiles[number + 1, slot]) + product(
                rows_left[:, slots:], tiles_of[number + 1]
            )
        for copy in out_copies(at, slot):
            copy.start()

        @pl.when((at >= first) & (at <= last))
        def _():
            place = pl.ds(pl.multiple_of((at - first) * tile, tile), tile)
            down_tiles[place] = product_left(own_tiles[0, slot], cots[:slots]) + product_left(
                tiles_of[0], cots[slots:]
            )

        return carry

    lax.fori_loop(0, tiles, each_tile, 0)
    offset = pl.multiple_of(replica * hidden_share - first * tile, 8)
    down_copy = pltpu.make_async_copy(down_tiles.at[pl.ds(offset, hidden_share)], down_out, down_sem)
    down_copy.start()
    for at in (tiles - 2, tiles - 1):
        for copy in out_copies(at, at % 2):
            copy.wait()
    for number in range(tiles + 2, summed.turns):
        summed.turn(number)
    down_copy.wait()


def last(sizes, number, shared, small, rows_in, cots_in, own_in, weights):
    n_dp, n_row, n_col = sizes
    normed = shared[0]
    tok, width = normed.shape
    hidden_width = weights[0].shape[1]
    slots = own_in[0].shape[0]
    total_rows = n_dp * slots
    tile = 256
    depth = width // (n_dp * n_row * n_col)
    strip = n_col * depth
    half, single = jnp.bfloat16, jnp.float32
    vmem, anywhere = pl.BlockSpec(memory_space=pltpu.VMEM), pl.BlockSpec(memory_space=pl.ANY)
    small = small.reshape(2, 2, n_row, strip, small.shape[1])
    hidden_share = hidden_width // n_dp
    spans = -(-hidden_share // tile) + 1
    scratch = [
        pltpu.VMEM((total_rows, width + LANES), half),
        pltpu.VMEM((total_rows, width), half),
        pltpu.VMEM((width // n_dp, total_rows), half),
        pltpu.VMEM((2, 2, width, tile), half),
        pltpu.VMEM((3, 2, slots, tile), half),
        pltpu.VMEM((3, total_rows - slots, tile), half),
        pltpu.VMEM((2, tile, width), half),
        pltpu.VMEM((2, 2, width // n_dp, tile), single),
        pltpu.VMEM((spans * tile, width), single),
    ]
    scratch += [pltpu.VMEM((2, 2, n_row, strip, width), half)] * 4
    for _ in range(4):
        scratch += share_scratch((n_row, n_col), depth, width, half)
    scratch += share_scratch((n_row, n_col), depth, LANES, single)
    sems = (5, 4 + n_col)
    scratch += [
        pltpu.SemaphoreType.DMA((2, 5)),
        pltpu.SemaphoreType.DMA((3, 2)),
        pltpu.SemaphoreType.DMA((3, 2)),
        pltpu.SemaphoreType.DMA((2, 2)),
        pltpu.SemaphoreType.DMA,
        pltpu.SemaphoreType.DMA(sems),
        pltpu.SemaphoreType.DMA(sems),
    ]
    out_shape = [jax.ShapeDtypeStruct((depth, width), single)] * 4
    out_shape += [jax.ShapeDtypeStruct((depth, LANES), single)]
    out_shape += [jax.ShapeDtypeStruct((width // n_dp, hidden_width), single)] * 2
    out_shape += [jax.ShapeDtypeStruct((hidden_share, width), single)]
    return pl.pallas_call(
        functools.partial(last_kernel, tile, (n_row, n_col), depth),
        out_shape=out_shape,
        in_specs=[vmem] * 7 + [anywhere] * 16,
        out_specs=[vmem] * 5 + [anywhere] * 3,
        scratch_shapes=scratch,
        compiler_params=pltpu.CompilerParams(
            collective_id=number, has_side_effects=True, vmem_limit_bytes=VMEM_LIMIT
        ),
    )(*shared, small, *rows_in, *cots_in, *own_in, *weights)


def gelu_parts(gate_part):
    square = gate_part * gate_part
    inner = gate_part * (0.7978845608028654 + 0.035677408136300125 * square)
    half = 0.5 + 0.5 * jnp.tanh(inner)
    value = gate_part * half
    slope = half + value * (1.0 - half) * (1.5957691216057308 + 0.21406444881780075 * square)
    return value, slope


def flat(*pieces):
    return [piece.reshape(-1, piece.shape[-1]) for piece in pieces]


def body(
    tokens,
    lengths,
    routes,
    attn_gain,
    query_weight,
    key_weight,
    value_weight,
    out_weight,
    relative_bias,
    moe_gain,
    router_weight,
    gate_weight,
    up_weight,
    down_weight,
    cotangent,
):
    tok_rows, width = tokens.shape[1:]
    head_count, bucket_count = relative_bias.shape
    expert_count = router_weight.shape[1]
    capacity = 5 * tok_rows // (2 * expert_count)
    room = -(-capacity // 16) * 16
    n_dp, n_row, n_col = (lax.axis_size(name) for name in ("dp", "erow", "ecol"))
    device_count = n_dp * n_row * n_col
    slot_count = expert_count * room
    gate_mat, up_mat, down_mat = gate_weight[0], up_weight[0], down_weight[0]
    near_routes = ((routes[0] % n_col) ^ lax.axis_index("ecol")) * n_row + (
        (routes[0] // n_col) ^ lax.axis_index("erow")
    )
    router = jnp.pad(router_weight, ((0, 0), (0, LANES - expert_count)))
    dims = (head_count, expert_count, room, capacity, n_row, n_col)
    normed, queries, both, probs, mixed, residual, gates, slot_rows, got_grads, near_grads = front(
        dims,
        0,
        lengths,
        tokens[0],
        cotangent[0],
        near_routes.T,
        routes[0],
        attn_gain[None],
        moe_gain[None],
        relative_bias,
        router,
        query_weight,
        key_weight,
        value_weight,
        out_weight,
    )
    (
        back,
        got,
        expert_out,
        own_hidden,
        own_gate_back,
        own_up_back,
        far_grads,
        near_grads_late,
        far_grads_late,
        near_rows,
        far_rows,
    ) = experts_apply((n_row, n_col), 1, slot_rows, got_grads, near_grads, gate_mat, up_mat, down_mat)
    depth = width // device_count
    bias_share = head_count * bucket_count // device_count
    output, token_grad, branch_grad, query_grad, key_grad, value_grad, small, near_rows_late, far_rows_late = backward(
        dims + (bias_share, depth),
        2,
        lengths,
        tokens[0],
        cotangent[0],
        near_routes,
        routes[0],
        attn_gain[None],
        moe_gain[None],
        router,
        residual,
        gates,
        mixed,
        probs,
        queries,
        both,
        back,
        expert_out,
        got,
        query_weight,
        key_weight,
        value_weight,
        out_weight,
    )
    out_sum, query_sum, key_sum, value_sum, small_sum, gate_total, up_total, down_total = last(
        (n_dp, n_row, n_col),
        3,
        (normed, query_grad, key_grad, value_grad, mixed, branch_grad),
        small,
        flat(got, near_rows, far_rows, near_rows_late, far_rows_late),
        flat(got_grads, near_grads, far_grads, near_grads_late, far_grads_late),
        (own_hidden, own_gate_back, own_up_back),
        (gate_mat, up_mat, down_mat),
    )
    return (
        output[None],
        token_grad[None],
        small_sum[:, LANES - 3],
        query_sum,
        key_sum,
        value_sum,
        out_sum,
        small_sum[:bias_share, LANES - 1],
        small_sum[:, LANES - 2],
        small_sum[:, :expert_count],
        gate_total[None],
        up_total[None],
        down_total[None],
    )


def solution(mesh):
    rows = P(("dp", "ecol"), "erow", None)
    experts = P(("erow", "ecol"), None, None)
    every = ("dp", "erow", "ecol")
    shares = P(("erow", "ecol"), "dp", None)
    return jax.shard_map(
        body,
        mesh=mesh,
        in_specs=(
            (rows, P(("dp", "ecol")), rows) + (P(),) * 8 + (experts, experts, experts, rows)
        ),
        out_specs=(rows, rows, P(every))
        + (P(every, None),) * 4
        + (P(every), P(every), P(every, None), shares, shares, shares),
        check_vma=False,
    )
```

profile of v0, /device:TPU:0, one launch (start us, length us, event | category | flops | bytes accessed | tf_op | source)
XLA Modules:
  0.0 275.0 jit_solution(9787580016560236078)
XLA Ops:
  1.3 0.8 copy.32
  2.1 0.0 copy-start
  2.1 0.1 fusion.8
  2.3 0.7 copy.34.routes_row
  2.9 0.8 fusion.2.near_col
  3.7 0.9 copy.33
  4.7 0.8 pad.4.router
  5.5 0.0 copy-done
  5.5 43.8 %shard_map.246 = (bf16[256,1024]{1,0:T(8,128)(2,1)}, bf16[256,1024]{1,0:T(8,128)(2,1)}, bf16[512,2048]{1,0:T(8,128)(2,1)}, bf16[16,256,512]{2,1,0:T(8,128)(2,1)}...) custom-call(s32[1]{0:T(128)S(6)} %copy.45.lengths, ...), custom_call_target="tpu_custom_call" | custom-call | tf_op jit(solution)/shard_map/pallas_call | solution.py:413
  49.3 77.6 %shard_map.247 = (bf16[8,80,1152]{2,1,0:T(8,128)(2,1)}, bf16[8,80,1152]{2,1,0:T(8,128)(2,1)}, bf16[8,80,1024]{2,1,0:T(8,128)(2,1)}, bf16[640,2816]{1,0:T(8,128)(...) custom-call(bf16[8,80,1152]{2,1,0:T(8,128)(2,1)} %get-tuple-element., ...), custom_call_target="tpu_custom_call" | custom-call | tf_op jit(solution)/shard_map/pallas_call | solution.py:611
  126.9 42.8 %shard_map.248 = (bf16[256,1024]{1,0:T(8,128)(2,1)}, f32[256,1024]{1,0:T(8,128)}, bf16[256,1024]{1,0:T(8,128)(2,1)}, bf16[256,1024]{1,0:T(8,128)(2,1)}, bf16[256...) custom-call(s32[1]{0:T(128)S(6)} %copy.45.lengths, ...), custom_call_target="tpu_custom_call" | custom-call | tf_op jit(solution)/shard_map/pallas_call | solution.py:890
  169.7 0.0 copy-start.5
  169.7 0.0 copy-start.4
  169.8 89.2 %shard_map.249 = (f32[32,1024]{1,0:T(8,128)}, f32[32,1024]{1,0:T(8,128)}, f32[32,1024]{1,0:T(8,128)}, f32[32,1024]{1,0:T(8,128)}, f32[32,128]{1,0:T(8,128)}, /*i...) custom-call(bf16[256,1024]{1,0:T(8,128)(2,1)} %get-tuple-element.65.refs_0_, ...), custom_call_target="tpu_custom_call" | custom-call | tf_op jit(solution)/shard_map/pallas_call | solution.py:1108
  258.9 0.0 copy-start.9
  259.0 1.4 slice_reduce_fusion.2
  260.4 1.5 slice_reduce_fusion
  261.9 1.4 copy.35
  263.3 0.0 copy-done.5
  263.3 0.8 copy.46
  264.1 1.0 copy.47
  265.1 0.0 copy-done.9
  265.1 0.7 copy.48
  265.7 0.0 copy-done.8
  265.7 0.7 copy.49
  266.4 0.7 copy.50
  267.1 0.7 copy.51
  267.7 1.6 copy.52
  269.3 1.3 copy-done.2
  270.6 1.6 copy.53
  272.1 1.3 copy-done.1
  273.4 1.6 copy.54
  (10 shorter events, 0.0 us)
Async XLA Ops:
  2.1 3.4 %copy-start = (s32[1,256,2]{2,1,0:T(8,128)}, s32[1,256,2]{2,1,0:T(8,128)S(1)}, u32[]{:S(2)}) copy-start(s32[1,256,2]{2,1,0:T(8,128)S(1)} %copy.32) | copy-start | bytes 6148
  169.7 93.6 %copy-start.5 = (bf16[256,1024]{1,0:T(8,128)(2,1)S(1)}, bf16[256,1024]{1,0:T(8,128)(2,1)}, u32[]{:S(2)}) copy-start(bf16[256,1024]{1,0:T(8,128)(2,1)} %get-tuple-element.63) | copy-start | bytes 1572868
  169.7 94.4 %copy-start.4 = (f32[256,1024]{1,0:T(8,128)S(1)}, f32[256,1024]{1,0:T(8,128)}, u32[]{:S(2)}) copy-start(f32[256,1024]{1,0:T(8,128)} %get-tuple-element.64) | copy-start | bytes 3145732
  258.9 6.1 %copy-start.9 = (f32[32,1024]{1,0:T(8,128)S(1)}, f32[32,1024]{1,0:T(8,128)}, u32[]{:S(2)}) copy-start(f32[32,1024]{1,0:T(8,128)} %get-tuple-element.133) | copy-start | bytes 393220
  258.9 6.8 %copy-start.8 = (f32[32,1024]{1,0:T(8,128)S(1)}, f32[32,1024]{1,0:T(8,128)}, u32[]{:S(2)}) copy-start(f32[32,1024]{1,0:T(8,128)} %get-tuple-element.134) | copy-start | bytes 393220
  259.0 7.4 %copy-start.7 = (f32[32,1024]{1,0:T(8,128)S(1)}, f32[32,1024]{1,0:T(8,128)}, u32[]{:S(2)}) copy-start(f32[32,1024]{1,0:T(8,128)} %get-tuple-element.135) | copy-start | bytes 393220
  259.0 8.1 %copy-start.6 = (f32[32,1024]{1,0:T(8,128)S(1)}, f32[32,1024]{1,0:T(8,128)}, u32[]{:S(2)}) copy-start(f32[32,1024]{1,0:T(8,128)} %get-tuple-element.136) | copy-start | bytes 393220
  263.3 4.4 %copy-start.3 = (f32[256,2816]{1,0:T(8,128)S(1)}, f32[256,2816]{1,0:T(8,128)}, u32[]{:S(2)}) copy-start(f32[256,2816]{1,0:T(8,128)} %get-tuple-element.86) | copy-start | bytes 8650756
  267.7 2.9 %copy-start.2 = (f32[256,2816]{1,0:T(8,128)S(1)}, f32[256,2816]{1,0:T(8,128)}, u32[]{:S(2)}) copy-start(f32[256,2816]{1,0:T(8,128)} %get-tuple-element.87) | copy-start | bytes 8650756
  270.6 2.9 %copy-start.1 = (f32[704,1024]{1,0:T(8,128)S(1)}, f32[704,1024]{1,0:T(8,128)}, u32[]{:S(2)}) copy-start(f32[704,1024]{1,0:T(8,128)} %get-tuple-element.88) | copy-start | bytes 8650756
where the time goes:
time: 280 us; the launch traced here: 275 us
  Pallas kernels  253 us (90%)
  local copies, waits for them, and re-layouts  19.3 us (7%)
    pallas_call x1, Pallas kernels, last(): pl.pallas_call(functools.partial(last_kernel, tile, (n_row, n_col), depth...  89.2 us
    pallas_call x1, Pallas kernels, experts_apply(): pl.pallas_call(functools.partial(expert_kernel, 256, sizes), out_shape=[j...  77.6 us
    pallas_call x1, Pallas kernels, front(): pl.pallas_call(functools.partial(front_kernel, dims), out_shape=[jax.Shap...  43.8 us
    pallas_call x1, Pallas kernels, backward(): pl.pallas_call(functools.partial(back_kernel, dims), out_shape=[jax.Shape...  42.8 us
    unnamed x32, local copies, waits for them, and re-layouts  14.8 us

commit v1 on v0

--- a/solution.py
+++ b/solution.py
@@ -64,10 +64,21 @@
     return index
 
 
+def mirrored(value, size):
+    result, bit = value * 0, 1
+    while bit < size:
+        result = result * 2 + (value // bit) % 2
+        bit *= 2
+    return result
+
+
 def partners(n_row, n_col):
     row, col = lax.axis_index("erow"), lax.axis_index("ecol")
     return [
-        {"erow": flipped(row, place % n_row, n_row), "ecol": flipped(col, place // n_row, n_col)}
+        {
+            "erow": flipped(row, place % n_row, n_row),
+            "ecol": flipped(col, mirrored(place // n_row, n_col), n_col),
+        }
         for place in range(n_row * n_col)
     ]
 
@@ -214,6 +225,11 @@
     return lax.broadcasted_iota(jnp.int32, shape, dimension)
 
 
+def columns_of(rows, count):
+    padded = jnp.concatenate([rows.astype(jnp.float32), jnp.zeros((8 - count, rows.shape[1]), jnp.float32)], axis=0)
+    return padded.T
+
+
 def row_slots(routes, live, experts, room, capacity):
     tok = live.shape[1]
     names = iota((experts, tok), 0)
@@ -249,7 +265,7 @@
     tokens,
     cotangent,
     routes_row,
-    routes_col,
+    routes_true,
     attn_gain,
     moe_gain,
     relative_bias,
@@ -268,6 +284,7 @@
     rows_out,
     cot_landed,
     cot_near,
+    cot_far,
     select,
     cot_slots,
     tables,
@@ -290,8 +307,8 @@
         load.start()
         loads.append(load)
     devices = partners(n_row, n_col)
-    spread = Spread(cot_near, None, near_send, near_recv)
-    part = len(devices) // 2
+    spread = Spread(cot_near, cot_far, near_send, near_recv)
+    part = len(devices) // 4
     barrier = pltpu.get_barrier_semaphore()
     for device in devices[1:] + spread.devices:
         pl.semaphore_signal(barrier, 1, device_id=device, device_id_type=MESH)
@@ -345,10 +362,15 @@
         value_lanes = pl.ds(pl.multiple_of(width + pair * pair_width, pair_width), pair_width)
         queries, keys, values = query_out[:, lanes], both_out[:, lanes], both_out[:, value_lanes]
 
-        @pl.when(pair == 1)
+        @pl.when(pair == 0)
         def _():
             wait_all([own] + copies[: part - 1])
             start_all(spread.first(cot_landed.at[pl.ds(0, part)]))
+
+        @pl.when(pair == heads // 4)
+        def _():
+            wait_all(spread.first(cot_landed.at[pl.ds(0, part)]))
+            start_all(spread.second())
 
         results = []
         for member in range(2):
@@ -371,15 +393,18 @@
     residual_out[...] = residual
     scale = lax.rsqrt(jnp.mean(residual * residual, axis=1, keepdims=True) + epsilon)
     moe_in = residual * scale * moe_gain[...]
-    logits = jnp.dot(moe_in, router[...], precision=highest, preferred_element_type=jnp.float32)
+    logits = lax.dot_general(
+        moe_in, router[...], (((1,), (1,)), ((), ())), precision=highest, preferred_element_type=jnp.float32
+    )
+    logits = jnp.concatenate([logits, jnp.full((tok, LANES - experts), -1e30, jnp.float32)], axis=1)
     lane = iota(logits.shape, 1)
-    logits = jnp.where(lane < experts, logits, -1e30)
+    columns = columns_of(routes_true[...], 2)
     powers = jnp.exp(logits - jnp.max(logits, axis=1, keepdims=True))
     gates = powers / jnp.sum(powers, axis=1, keepdims=True)
     gates_out[...] = gates
     panel = jnp.zeros((experts * room, LANES), jnp.float32)
     for k in range(2):
-        pick = jnp.sum(jnp.where(routes_col[:, k : k + 1] == lane, gates, 0.0), axis=1, keepdims=True)
+        pick = jnp.sum(jnp.where(columns[:, k : k + 1] == lane.astype(jnp.float32), gates, 0.0), axis=1, keepdims=True)
         high = pick.astype(jnp.bfloat16)
         low = (pick - high.astype(jnp.float32)).astype(jnp.bfloat16)
         parts = jnp.where(lane == 0, high, jnp.where(lane == 1, low, jnp.zeros_like(low)))
@@ -388,7 +413,7 @@
     rows_out[:, :, :width] = rows.astype(jnp.bfloat16).reshape(rows_out.shape[0], -1, width)
     rows_out[:, :, width:] = panel.astype(jnp.bfloat16).reshape(rows_out.shape[0], -1, LANES)
     wait_all(copies[part - 1 :])
-    wait_all(spread.first(cot_landed.at[pl.ds(0, part)]))
+    wait_all(spread.second())
 
 
 def front(dims, number, lengths, tokens, cotangent, routes_row, routes_col, *params):
@@ -408,13 +433,14 @@
         ((tok, LANES), single),
         ((group, blocks, width + LANES), half),
         ((group, blocks, width), half),
-        ((2, group // 2, blocks, width), half),
+        ((2, group // 4, blocks, width), half),
+        ((group // 4, blocks, width), half),
     ]
     return pl.pallas_call(
         functools.partial(front_kernel, dims),
         out_shape=[jax.ShapeDtypeStruct(shape, kind) for shape, kind in shapes],
         in_specs=[pl.BlockSpec(memory_space=pltpu.SMEM)] + [vmem] * 8 + [anywhere] * 4,
-        out_specs=[vmem] * 8 + [anywhere] * 2,
+        out_specs=[vmem] * 8 + [anywhere] * 3,
         scratch_shapes=[
             pltpu.VMEM((experts * room, tok), half),
             pltpu.VMEM((group, blocks, width), half),
@@ -426,8 +452,8 @@
             pltpu.SemaphoreType.DMA((group - 1,)),
             pltpu.SemaphoreType.DMA,
             pltpu.SemaphoreType.DMA,
-            pltpu.SemaphoreType.DMA((2,)),
-            pltpu.SemaphoreType.DMA((2,)),
+            pltpu.SemaphoreType.DMA((4,)),
+            pltpu.SemaphoreType.DMA((4,)),
         ],
         compiler_params=pltpu.CompilerParams(
             collective_id=number, has_side_effects=True, vmem_limit_bytes=VMEM_LIMIT
@@ -435,43 +461,58 @@
     )(lengths, tokens, cotangent, routes_row, routes_col, *params)
 
 
+def panel_sum(panel):
+    return panel[:, 0:1].astype(jnp.float32) + panel[:, 1:2].astype(jnp.float32)
+
+
 def expert_kernel(
     tile,
     sizes,
     rows_sent,
     cot_own,
-    cot_near,
+    cot_near0,
+    cot_far0,
     gate_weight,
     up_weight,
     down_weight,
     back_landed,
     rows_landed,
     out_rows,
-    hidden_all,
-    gate_back_all,
-    up_back_all,
-    cot_far,
-    cot_near_late,
-    cot_far_late,
-    rows_near,
-    rows_far,
+    parts_out,
+    cot_near1,
+    cot_far1,
+    cot_near2,
+    cot_far2,
+    cot_near3,
+    cot_far3,
+    rows_near0,
+    rows_far0,
+    rows_near1,
+    rows_far1,
     gate_mat,
     up_mat,
     down_mat,
     cot,
     down_rows,
+    hidden_all,
     total,
     picks_back,
     back_sent,
+    other_rows,
+    other_cots,
+    staged,
     load_sems,
     own_sems,
     send_sems,
     recv_sems,
     spread_send,
     spread_recv,
+    stage_sems,
+    other_sems,
 ):
     group, room, width = cot_own.shape
     hidden_width = gate_mat.shape[1]
+    tiles = hidden_width // tile
     loads = []
     for at, (source, target) in enumerate(
         ((cot_own, cot), (down_weight, down_mat), (gate_weight, gate_mat), (up_weight, up_mat))
@@ -480,33 +521,131 @@
         load.start()
         loads.append(load)
     devices = partners(*sizes)
-    part = group // 2
-    spreads = [
+    part, quarter = group // 2, group // 4
+    strip = part * room
+    cot_spreads = [None] + [
         Spread(near, far, spread_send.at[at], spread_recv.at[at])
-        for at, (near, far) in enumerate(((cot_near, cot_far), (cot_near_late, cot_far_late), (rows_near, rows_far)))
+        for at, (near, far) in enumerate(((cot_near1, cot_far1), (cot_near2, cot_far2), (cot_near3, cot_far3)))
     ]
-    late_cots = cot_own.at[pl.ds(part, part)]
-    early_rows = rows_landed.at[pl.ds(0, part)]
-    greet(devices[1:] + spreads[0].devices)
-    copies = {}
-    for place in range(group):
+    row_spreads = [
+        Spread(near, far, spread_send.at[3 + at], spread_recv.at[3 + at])
+        for at, (near, far) in enumerate(((rows_near0, rows_far0), (rows_near1, rows_far1)))
+    ]
+    greet(devices[1:] + row_spreads[0].devices)
+
+    def cots_first(piece):
+        return cot_spreads[piece].first(cot_own.at[pl.ds(piece * quarter, quarter)])
+
+    def rows_first(piece):
+        return row_spreads[piece].first(rows_landed.at[pl.ds(piece * quarter, quarter)])
+
+    def row_copy(way, place):
+        source, target = ((rows_sent, rows_landed), (back_sent, back_landed))[way]
         if place == 0:
-            copy = pltpu.make_async_copy(rows_sent.at[0], rows_landed.at[0], own_sems.at[0])
-        else:
-            copy = remote(
-                rows_sent.at[place],
-                rows_landed.at[place],
-                send_sems.at[0, place - 1],
-                recv_sems.at[0, place - 1],
-                devices[place],
+            return pltpu.make_async_copy(source.at[0], target.at[0], own_sems.at[way])
+        sems = (send_sems.at[way, place - 1], recv_sems.at[way, place - 1])
+        return remote(source.at[place], target.at[place], *sems, devices[place])
+
+    def stage_copy(at, slot, start, size):
+        return pltpu.make_async_copy(
+            staged.at[slot, :, pl.ds(0, size)], parts_out.at[at, :, pl.ds(start, size)], stage_sems.at[slot]
+        )
+
+    def stage_free(at, start, size):
+        @pl.when(at >= 2)
+        def _():
+            stage_copy(at - 2, lax.rem(at, 2), start, size).wait()
+
+    def stage(at, start, size, hidden, gate_back, up_back):
+        slot = lax.rem(at, 2)
+        for number, values in enumerate((hidden, gate_back, up_back)):
+            staged[slot, number, pl.ds(0, size)] = values
+        return stage_copy(at, slot, start, size)
+
+    def stage_end(start, size):
+        for at in (tiles - 2, tiles - 1):
+            stage_copy(at, at % 2, start, size).wait()
+
+    def own_half(half):
+        held = slice(half * part, (half + 1) * part)
+        cut_rows = pl.ds(half * strip, strip)
+        rows = rows_landed[held, :, :width].reshape(strip, width)
+        picks = panel_sum(rows_landed[held, :, width:].reshape(strip, LANES))
+        total[...] = jnp.zeros_like(total)
+        picks_back[...] = jnp.zeros_like(picks_back)
+
+        def middle(at, carry):
+            stage_free(at, half * strip, strip)
+            cut = pl.ds(pl.multiple_of(at * tile, tile), tile)
+            value, slope = gelu_parts(product(rows, gate_mat[:, cut]))
+            up_part = product(rows, up_mat[:, cut])
+            hidden = value * up_part
+            hidden_low = hidden.astype(jnp.bfloat16)
+            hidden_all[cut_rows, cut] = hidden_low
+            back = down_rows[cut_rows, cut].astype(jnp.float32)
+            weighed = hidden * back
+            picks_back[...] += sum(weighed[:, lane : lane + LANES] for lane in range(0, tile, LANES))
+            back = back * picks
+            gate_back = (back * up_part * slope).astype(jnp.bfloat16)
+            up_back = (back * value).astype(jnp.bfloat16)
+            store = stage(at, half * strip, strip, hidden_low, gate_back, up_back)
+            total[...] += product_back(
+                jnp.concatenate([gate_back, up_back], axis=1),
+                jnp.concatenate([gate_mat[:, cut], up_mat[:, cut]], axis=1),
             )
-        copy.start()
-        copies[0, place] = copy
-    start_all(spreads[0].second())
-    start_all(spreads[1].first(late_cots))
-    tiles = hidden_width // tile
-    loads[0].wait()
-    loads[1].wait()
+            store.start()
+            return carry
+
+        lax.fori_loop(0, tiles, middle, 0)
+        back_sent[held, :, :width] = total[...].astype(jnp.bfloat16).reshape(part, room, width)
+        high, low = halves(jnp.sum(picks_back[...], axis=1, keepdims=True))
+        lane = iota((strip, LANES), 1)
+        panel = jnp.where(lane == 0, high, jnp.where(lane == 1, low, jnp.zeros_like(low)))
+        back_sent[held, :, width:] = panel.reshape(part, room, LANES)
+        start_all([row_copy(1, place) for place in range(half * part, (half + 1) * part)])
+        stage_end(half * strip, strip)
+
+    def others(start, sources):
+        at, copies = 0, []
+        for number, (row_source, cot_source) in enumerate(sources):
+            size = row_source.shape[0]
+            place = pl.ds(at, size)
+            copies += [
+                pltpu.make_async_copy(row_source, other_rows.at[place], other_sems.at[0, number]),
+                pltpu.make_async_copy(cot_source, other_cots.at[place], other_sems.at[1, number]),
+            ]
+            at += size
+        size = at
+        start_all(copies)
+        wait_all(copies)
+        rows = other_rows[:size, :, :width].reshape(size * room, width)
+        picks = panel_sum(other_rows[:size, :, width:].reshape(size * room, LANES))
+        cots = (other_cots[:size].reshape(size * room, width).astype(jnp.float32) * picks).astype(jnp.bfloat16)
+        size = size * room
+
+        def middle(at, carry):
+            stage_free(at, start, size)
+            cut = pl.ds(pl.multiple_of(at * tile, tile), tile)
+            value, slope = gelu_parts(product(rows, gate_mat[:, cut]))
+            up_part = product(rows, up_mat[:, cut])
+            back = product_back(cots, down_mat[cut, :])
+            store = stage(
+                at,
+                start,
+                size,
+                (value * up_part).astype(jnp.bfloat16),
+                (back * up_part * slope).astype(jnp.bfloat16),
+                (back * value).astype(jnp.bfloat16),
+            )
+            store.start()
+            return carry
+
+        lax.fori_loop(0, tiles, middle, 0)
+        stage_end(start, size)
+
+    start_all([row_copy(0, place) for place in range(part)])
+    start_all(cots_first(1))
+    wait_all(loads[:2])
     cot_rows = cot[...].reshape(group * room, width)
 
     def early(at, carry):
@@ -515,66 +654,27 @@
         return carry
 
     lax.fori_loop(0, tiles, early, 0)
-    loads[2].wait()
-    loads[3].wait()
-    for half in range(2):
-        places = range(half * part, (half + 1) * part)
-        for place in places:
-            copies[0, place].wait()
-        if half == 0:
-            start_all(spreads[2].first(early_rows))
-        held = slice(half * part, (half + 1) * part)
-        strip = slice(half * part * room, (half + 1) * part * room)
-        rows = rows_landed[held, :, :width].reshape(part * room, width)
-        panel = rows_landed[held, :, width:].reshape(part * room, LANES)
-        picks = panel[:, 0:1].astype(jnp.float32) + panel[:, 1:2].astype(jnp.float32)
-        total[...] = jnp.zeros_like(total)
-        picks_back[...] = jnp.zeros_like(picks_back)
-
-        def middle(at, carry):
-            cut = pl.ds(pl.multiple_of(at * tile, tile), tile)
-            value, slope = gelu_parts(product(rows, gate_mat[:, cut]))
-            up_part = product(rows, up_mat[:, cut])
-            hidden = value * up_part
-            hidden_all[strip, cut] = hidden.astype(jnp.bfloat16)
-            back = down_rows[strip, cut].astype(jnp.float32)
-            weighed = hidden * back
-            picks_back[...] += sum(weighed[:, at : at + LANES] for at in range(0, tile, LANES))
-            back = back * picks
-            gate_back = (back * up_part * slope).astype(jnp.bfloat16)
-            up_back = (back * value).astype(jnp.bfloat16)
-            gate_back_all[strip, cut] = gate_back
-            up_back_all[strip, cut] = up_back
-            total[...] += product_back(gate_back, gate_mat[:, cut]) + product_back(up_back, up_mat[:, cut])
-            return carry
-
-        lax.fori_loop(0, tiles, middle, 0)
-        back_sent[held, :, :width] = total[...].astype(jnp.bfloat16).reshape(part, room, width)
-        pick = jnp.sum(picks_back[...], axis=1, keepdims=True)
-        high = pick.astype(jnp.bfloat16)
-        low = (pick - high.astype(jnp.float32)).astype(jnp.bfloat16)
-        lane = iota((part * room, LANES), 1)
-        parts = jnp.where(lane == 0, high, jnp.where(lane == 1, low, jnp.zeros_like(low)))
-        back_sent[held, :, width:] = parts.reshape(part, room, LANES)
-        for place in places:
-            if place == 0:
-                copy = pltpu.make_async_copy(back_sent.at[0], back_landed.at[0], own_sems.at[1])
-            else:
-                copy = remote(
-                    back_sent.at[place],
-                    back_landed.at[place],
-                    send_sems.at[1, place - 1],
-                    recv_sems.at[1, place - 1],
-                    devices[place],
-                )
-            copy.start()
-            copies[1, place] = copy
-        if half == 0:
-            wait_all(spreads[1].first(late_cots))
-            start_all(spreads[1].second())
-        else:
-            wait_all(spreads[2].first(early_rows))
-            start_all(spreads[2].second())
+    wait_all(loads[2:])
+    wait_all([row_copy(0, place) for place in range(quarter)])
+    start_all(rows_first(0))
+    wait_all([row_copy(0, place) for place in range(quarter, part)])
+    start_all([row_copy(0, place) for place in range(part, group)])
+    start_all(rows_first(1))
+    own_half(0)
+    wait_all(cots_first(1) + rows_first(0))
+    start_all(cot_spreads[1].second() + row_spreads[0].second() + cots_first(2))
+    others(2 * strip, [(rows_near0.at[k], cot_near0.at[k]) for k in range(2)])
+    wait_all(rows_first(1))
+    start_all(row_spreads[1].second() + cots_first(3))
+    wait_all([row_copy(0, place) for place in range(part, group)])
+    own_half(1)
+    wait_all(cots_first(2) + cots_first(3))
+    start_all(cot_spreads[2].second() + cot_spreads[3].second())
+    wait_all(cot_spreads[1].second() + row_spreads[0].second() + row_spreads[1].second())
+    others(
+        3 * strip,
+        [(rows_near1.at[k], cot_near1.at[k]) for k in range(2)] + [(rows_far0, cot_far0), (rows_far1, cot_far1)],
+    )
 
     def outward(at, carry):
         cut = pl.ds(pl.multiple_of(at * tile, tile), tile)
@@ -583,61 +683,58 @@
         return carry
 
     lax.fori_loop(0, width // tile, outward, 0)
-    for place in range(group):
-        copies[1, place].wait()
-    for spread in spreads:
-        wait_all(spread.second())
-
-
-def experts_apply(sizes, number, rows_sent, cot_own, cot_near, gate_weight, up_weight, down_weight):
+    wait_all([row_copy(1, place) for place in range(group)])
+    wait_all(cot_spreads[2].second() + cot_spreads[3].second())
+
+
+def experts_apply(sizes, number, tile, *operands):
+    rows_sent, cot_own = operands[:2]
     group, room, width = cot_own.shape
-    hidden_width = gate_weight.shape[1]
+    hidden_width = operands[4].shape[1]
     slots = group * room
+    quarter = group // 4
     half, single = jnp.bfloat16, jnp.float32
     vmem, anywhere = pl.BlockSpec(memory_space=pltpu.VMEM), pl.BlockSpec(memory_space=pl.ANY)
-    shapes = [
-        rows_sent.shape,
-        rows_sent.shape,
-        cot_own.shape,
-        (slots, hidden_width),
-        (slots, hidden_width),
-        (slots, hidden_width),
-        (group // 2, room, width),
-        (2, group // 2, room, width),
-        (group // 2, room, width),
-        (2, group // 2, room, rows_sent.shape[2]),
-        (group // 2, room, rows_sent.shape[2]),
-    ]
+    wide = rows_sent.shape[2]
+    shapes = [rows_sent.shape, rows_sent.shape, cot_own.shape, (hidden_width // tile, 3, 5 * slots // 2, tile)]
+    shapes += [(2, quarter, room, width), (quarter, room, width)] * 3
+    shapes += [(2, quarter, room, wide), (quarter, room, wide)] * 2
     return pl.pallas_call(
-        functools.partial(expert_kernel, 256, sizes),
+        functools.partial(expert_kernel, tile, sizes),
         out_shape=[jax.ShapeDtypeStruct(shape, half) for shape in shapes],
-        in_specs=[anywhere] * 6,
-        out_specs=[anywhere] + [vmem] * 5 + [anywhere] * 5,
+        in_specs=[anywhere] * 7,
+        out_specs=[anywhere] + [vmem] * 2 + [anywhere] * 11,
         scratch_shapes=[
             pltpu.VMEM((width, hidden_width), half),
             pltpu.VMEM((width, hidden_width), half),
             pltpu.VMEM((hidden_width, width), half),
             pltpu.VMEM((group, room, width), half),
             pltpu.VMEM((slots, hidden_width), half),
+            pltpu.VMEM((slots, hidden_width), half),
             pltpu.VMEM((slots // 2, width), single),
             pltpu.VMEM((slots // 2, LANES), single),
             pltpu.VMEM(rows_sent.shape, half),
+            pltpu.VMEM((4 * quarter, room, wide), half),
+            pltpu.VMEM((4 * quarter, room, width), half),
+            pltpu.VMEM((2, 3, slots, tile), half),
             pltpu.SemaphoreType.DMA((4,)),
             pltpu.SemaphoreType.DMA((2,)),
             pltpu.SemaphoreType.DMA((2, group - 1)),
             pltpu.SemaphoreType.DMA((2, group - 1)),
-            pltpu.SemaphoreType.DMA((3, 4)),
-            pltpu.SemaphoreType.DMA((3, 4)),
+            pltpu.SemaphoreType.DMA((5, 4)),
+            pltpu.SemaphoreType.DMA((5, 4)),
+            pltpu.SemaphoreType.DMA((2,)),
+            pltpu.SemaphoreType.DMA((2, 4)),
         ],
         compiler_params=pltpu.CompilerParams(
             collective_id=number, has_side_effects=True, vmem_limit_bytes=VMEM_LIMIT
         ),
-    )(rows_sent, cot_own, cot_near, gate_weight, up_weight, down_weight)
+    )(*operands)
 
 
 def column_slots(routes, live, experts, room, capacity):
     tok = live.shape[0]
-    names = iota((tok, experts), 1)
+    names = iota((tok, experts), 1).astype(jnp.float32)
     hot = [(routes[:, k : k + 1] == names) & live for k in range(2)]
     both = jnp.where(hot[0] | hot[1], 1.0, 0.0).astype(jnp.bfloat16)
     before = jnp.where(iota((tok, tok), 1) < iota((tok, tok), 0), 1.0, 0.0).astype(jnp.bfloat16)
@@ -645,7 +742,7 @@
     slots = []
     for k in range(2):
         place = jnp.sum(jnp.where(hot[k], earlier, 0.0), axis=1, keepdims=True)
-        slot = routes[:, k : k + 1].astype(jnp.float32) * room + place
+        slot = routes[:, k : k + 1] * room + place
         slots.append(jnp.where(live & (place < capacity), slot, -1.0))
     return slots
 
@@ -660,8 +757,8 @@
     lengths,
     tokens,
     cotangent,
-    near_col,
-    routes_col,
+    near_row,
+    routes_true,
     attn_gain,
     moe_gain,
     router,
@@ -672,23 +769,22 @@
     queries_in,
     both,
     back_in,
-    out_sent,
     rows_own,
     query_weight,
     key_weight,
     value_weight,
     out_weight,
-    output,
     token_grad,
-    branch_grad,
     query_grad,
     key_grad,
     value_grad,
     small,
-    rows_near,
-    rows_far,
+    rows_near2,
+    rows_far2,
+    rows_near3,
+    rows_far3,
+    out_total,
     back,
-    out_landed,
     held_weights,
     mixed_back,
     residual_grad,
@@ -697,14 +793,14 @@
     near_sum,
     diagonals,
     load_sems,
-    own_sem,
-    send_sems,
-    recv_sems,
     row_send,
     row_recv,
     near_send,
     near_recv,
+    out_wgrad,
+    *shared,
 ):
+    *held, sum_send, sum_recv = shared
     heads, experts, room, capacity, n_row, n_col, share, depth = dims
     tok, width = tokens.shape
     pair_width = 2 * width // heads
@@ -719,32 +815,26 @@
         load.start()
         loads.append(load)
     devices = partners(n_row, n_col)
-    spread = Spread(rows_near, rows_far, near_send, near_recv)
-    part = len(devices) // 2
-    late_rows = rows_own.at[pl.ds(part, part)]
-    greet(devices[1:] + spread.devices)
-    start_all(spread.first(late_rows))
-    copies = [pltpu.make_async_copy(out_sent.at[0], out_landed.at[0], own_sem)]
-    for place in range(1, len(devices)):
-        copies.append(
-            remote(
-                out_sent.at[place],
-                out_landed.at[place],
-                send_sems.at[place - 1],
-                recv_sems.at[place - 1],
-                devices[place],
-            )
-        )
-    for copy in copies:
-        copy.start()
-
+    spreads = [
+        Spread(near, far, near_send.at[at], near_recv.at[at])
+        for at, (near, far) in enumerate(((rows_near2, rows_far2), (rows_near3, rows_far3)))
+    ]
+    quarter = len(devices) // 4
+    summed = ShareSum((n_row, n_col), depth, [out_wgrad], [out_total], [held], sum_send, sum_recv)
+    greet(devices[1:] + spreads[0].devices)
+
+    def rows_first(at):
+        return spreads[at].first(rows_own.at[pl.ds((2 + at) * quarter, quarter)])
+
+    start_all(rows_first(0))
     piece = lax.axis_index("erow")
     live = iota((tok, 1), 0) + piece * tok < lengths[0]
-    slots = column_slots(near_col[...], live, experts, room, capacity)
+    slots = column_slots(columns_of(near_row[...], 2), live, experts, room, capacity)
     names = iota((tok, slots_count), 1).astype(jnp.float32)
     hot = [jnp.where(names == slot, 1.0, 0.0).astype(jnp.bfloat16) for slot in slots]
     lane = iota((tok, LANES), 1)
-    chosen = [routes_col[:, k : k + 1] == lane for k in range(2)]
+    columns = columns_of(routes_true[...], 2)
+    chosen = [columns[:, k : k + 1] == lane.astype(jnp.float32) for k in range(2)]
     gates = gates_in[...]
 
     residual = residual_in[...]
@@ -759,11 +849,12 @@
     logit_back = gates * (prob_back - jnp.sum(gates * prob_back, axis=1, keepdims=True))
     logit_high, logit_low = halves(logit_back)
     router_high, router_low = halves(router[...])
+    few = slice(0, experts)
     moe_back = (
         product(hot[0] + hot[1], back[:, :, :width].reshape(slots_count, width))
-        + product_back(logit_high, router_high)
-        + product_back(logit_low, router_high)
-        + product_back(logit_high, router_low)
+        + product(logit_high[:, few], router_high)
+        + product(logit_low[:, few], router_high)
+        + product(logit_high[:, few], router_low)
     )
     left = moe_in.T
     router_grad = product(left, logit_high) + product(left, logit_low)
@@ -776,9 +867,10 @@
     )
     residual_grad[...] = total
     branch = total.astype(jnp.bfloat16)
-    branch_grad[...] = branch
     loads[1].wait()
     mixed_back[...] = product_back(branch, held_weights[0]).astype(jnp.bfloat16)
+    out_wgrad[...] = product(mixed[...].T, branch).astype(jnp.bfloat16).reshape(out_wgrad.shape)
+    summed.turn(0)
     reversal = jnp.where(iota((tok, tok), 0) + iota((tok, tok), 1) == tok - 1, 1.0, 0.0).astype(jnp.bfloat16)
     low_half = iota((tok, pair_width), 1) < member_width
 
@@ -788,10 +880,22 @@
         keys, values = both[:, lanes], both[:, value_lanes]
         grads = mixed_back[:, lanes]
 
-        @pl.when(pair == heads // 2 - 2)
+        @pl.when(pair == 1)
         def _():
-            wait_all(spread.first(late_rows))
-            start_all(spread.second())
+            summed.turn(1)
+
+        @pl.when(pair == 3)
+        def _():
+            wait_all(rows_first(0))
+            start_all(spreads[0].second() + rows_first(1))
+
+        @pl.when(pair == 5)
+        def _():
+            summed.turn(2)
+
+        @pl.when(pair == heads // 2 - 1)
+        def _():
+            summed.turn(3)
 
         queries_left, grads_left = queries_in[:, lanes].T, grads.T
         query_parts, key_parts, value_parts = [], [], []
@@ -850,6 +954,8 @@
     pair_copy.wait()
     key_total = (near_sum[:, :width] + far_landed[:, :width].astype(jnp.float32)).astype(jnp.bfloat16)
     value_total = (near_sum[:, width:] + far_landed[:, width:].astype(jnp.float32)).astype(jnp.bfloat16)
+    wait_all(rows_first(1))
+    start_all(spreads[1].second())
     key_grad[...] = key_total
     value_grad[...] = value_total
     loads[3].wait()
@@ -866,35 +972,28 @@
     )
     empty = jnp.zeros((LANES - 3, width), jnp.float32)
     small[...] = jnp.concatenate([empty, attn_gain_grad, moe_gain_grad, bias_row], axis=0).T + router_grad
-
-    for copy in copies:
-        copy.wait()
-    results = out_landed[...].reshape(slots_count, width)
-    total = residual
-    for k in range(2):
-        pick = jnp.sum(jnp.where(chosen[k], gates, 0.0), axis=1, keepdims=True)
-        total = total + pick * product(hot[k], results)
-    output[...] = total.astype(jnp.bfloat16)
-    wait_all(spread.second())
+    wait_all(spreads[0].second() + spreads[1].second())
+    summed.turn(4)
 
 
 def backward(dims, number, *operands):
     heads, experts, room, capacity, n_row, n_col, share, depth = dims
-    tokens, back_in, out_sent, rows_own = operands[1], operands[14], operands[15], operands[16]
+    tokens, back_in, rows_own = operands[1], operands[14], operands[15]
     tok, width = tokens.shape
     group = n_row * n_col
     half, single = jnp.bfloat16, jnp.float32
     vmem, anywhere = pl.BlockSpec(memory_space=pltpu.VMEM), pl.BlockSpec(memory_space=pl.ANY)
-    shapes = [((tok, width), half), ((tok, width), single)] + [((tok, width), half)] * 4 + [((width, LANES), single)]
-    shapes += [((2, group // 2) + rows_own.shape[1:], half), ((group // 2,) + rows_own.shape[1:], half)]
+    shapes = [((tok, width), single)] + [((tok, width), half)] * 3 + [((width, LANES), single)]
+    shapes += [((2, group // 4) + rows_own.shape[1:], half), ((group // 4,) + rows_own.shape[1:], half)] * 2
+    shapes += [((depth, width), single)]
+    sems = (1, 4 + n_col)
     return pl.pallas_call(
         functools.partial(back_kernel, dims),
         out_shape=[jax.ShapeDtypeStruct(shape, kind) for shape, kind in shapes],
-        in_specs=[pl.BlockSpec(memory_space=pltpu.SMEM)] + [vmem] * 13 + [anywhere] * 7,
-        out_specs=[vmem] * 7 + [anywhere] * 2,
+        in_specs=[pl.BlockSpec(memory_space=pltpu.SMEM)] + [vmem] * 13 + [anywhere] * 6,
+        out_specs=[vmem] * 5 + [anywhere] * 4 + [vmem],
         scratch_shapes=[
             pltpu.VMEM(back_in.shape, half),
-            pltpu.VMEM(out_sent.shape, half),
             pltpu.VMEM((4, width, width), half),
             pltpu.VMEM((tok, width), half),
             pltpu.VMEM((tok, width), single),
@@ -904,41 +1003,45 @@
             pltpu.VMEM((heads, 4 * tok), single),
             pltpu.SemaphoreType.DMA((5,)),
             pltpu.SemaphoreType.DMA,
-            pltpu.SemaphoreType.DMA((group - 1,)),
-            pltpu.SemaphoreType.DMA((group - 1,)),
             pltpu.SemaphoreType.DMA,
-            pltpu.SemaphoreType.DMA,
-            pltpu.SemaphoreType.DMA((4,)),
-            pltpu.SemaphoreType.DMA((4,)),
-        ],
+            pltpu.SemaphoreType.DMA((2, 4)),
+            pltpu.SemaphoreType.DMA((2, 4)),
+            pltpu.VMEM((2, 2, n_row, n_col * depth, width), half),
+        ]
+        + share_scratch((n_row, n_col), depth, width, half)
+        + [pltpu.SemaphoreType.DMA(sems), pltpu.SemaphoreType.DMA(sems)],
         compiler_params=pltpu.CompilerParams(
             collective_id=number, has_side_effects=True, vmem_limit_bytes=VMEM_LIMIT
         ),
     )(*operands)
 
 
-def last_kernel(tile, sizes, depth, *refs):
-    pieces = 5
-    (normed, query_grad, key_grad, value_grad, mixed, branch_grad, small), refs = refs[:7], refs[7:]
+def last_kernel(tile, sizes, depth, slot_sizes, *refs):
+    pieces = 9
+    (lengths, near_row, routes_true, residual, gates_in), refs = refs[:5], refs[5:]
+    (normed, query_grad, key_grad, value_grad, small), refs = refs[:5], refs[5:]
     rows_in, refs = refs[:pieces], refs[pieces:]
     cots_in, refs = refs[:pieces], refs[pieces:]
-    (own_in, weights, sums), refs = (refs[:3], refs[3:6], refs[6:11]), refs[11:]
-    (gate_out, up_out, down_out), refs = refs[:3], refs[3:]
-    (rows, cots, rows_left, mats, own_tiles, tiles_of, own_mats, out_tiles, down_tiles), refs = refs[:9], refs[9:]
-    grads, refs = refs[:4], refs[4:]
-    held, refs = [refs[5 * at : 5 * at + 5] for at in range(5)], refs[25:]
+    parts_in, out_sent, weights, sums, refs = refs[0], refs[1], refs[2:5], refs[5:9], refs[9:]
+    (gate_out, up_out, down_out, output), refs = refs[:4], refs[4:]
+    (out_landed, out_own, out_send, out_recv), refs = refs[:4], refs[4:]
+    (rows, cots, rows_left, mats, tiles_of, own_mats, out_tiles, down_tiles), refs = refs[:8], refs[8:]
+    grads, refs = refs[:3], refs[3:]
+    held, refs = [refs[5 * at : 5 * at + 5] for at in range(4)], refs[20:]
     load_sems, weight_sems, own_sems, out_sems, down_sem, send_sems, recv_sems = refs
     width, strip = normed.shape[1], grads[0].shape[3]
     hidden_width = weights[0].shape[1]
     tiles = hidden_width // tile
-    slots = own_in[0].shape[0]
+    ready = parts_in.shape[2]
     total_rows = rows.shape[0]
+    chunk = (total_rows - ready) // 2
     share = width // 4
     hidden_share = hidden_width // 4
     replica = lax.axis_index("dp")
     summed = ShareSum(sizes, depth, list(grads) + [small], sums, held, send_sems, recv_sems)
     barrier = pltpu.get_barrier_semaphore()
-    for device in summed.devices:
+    devices = partners(*sizes)
+    for device in devices[1:] + summed.devices[1:3]:
         pl.semaphore_signal(barrier, 1, device_id=device, device_id_type=MESH)
     loads, start = [], 0
     for at, (row_piece, cot_piece) in enumerate(zip(rows_in, cots_in)):
@@ -957,12 +1060,8 @@
         ] + [pltpu.make_async_copy(weights[2].at[cut], own_mats.at[slot], weight_sems.at[2, slot])]
 
     def own_loads(at, slot):
-        cut = pl.ds(pl.multiple_of(at * tile, tile), tile)
         return [
-            pltpu.make_async_copy(
-                source.at[:, cut], own_tiles.at[number, slot], own_sems.at[number, slot]
-            )
-            for number, source in enumerate(own_in)
+            pltpu.make_async_copy(parts_in.at[at], tiles_of.at[slot, :, pl.ds(0, ready)], own_sems.at[slot])
         ]
 
     def out_copies(at, slot):
@@ -972,17 +1071,25 @@
             for number, target in enumerate((gate_out, up_out))
         ]
 
-    for load in weight_loads(0, 0) + own_loads(0, 0):
-        load.start()
-    left = mixed[...].T
+    first = lax.div(replica * hidden_share, tile)
+    spans = lax.div((replica + 1) * hidden_share - 1, tile) - first + 1
+
+    def tile_at(turn):
+        return lax.rem(first + turn, tiles)
+
+    start_all(weight_loads(tile_at(0), 0) + own_loads(tile_at(0), 0))
+    left = normed[...].T
     shape = grads[0].shape
-    grads[0][...] = product(left, branch_grad[...]).astype(jnp.bfloat16).reshape(shape)
-    left = normed[...].T
-    pl.semaphore_wait(barrier, len(summed.devices))
+    grads[0][...] = product(left, query_grad[...]).astype(jnp.bfloat16).reshape(shape)
+    pl.semaphore_wait(barrier, len(devices) + 1)
+    returns = [pltpu.make_async_copy(out_sent.at[0], out_landed.at[0], out_own)]
+    for place in range(1, len(devices)):
+        sems = (out_send.at[place - 1], out_recv.at[place - 1])
+        returns.append(remote(out_sent.at[place], out_landed.at[place], *sems, devices[place]))
+    start_all(returns)
     summed.turn(0)
-    grads[1][...] = product(left, query_grad[...]).astype(jnp.bfloat16).reshape(shape)
-    grads[2][...] = product(left, key_grad[...]).astype(jnp.bfloat16).reshape(shape)
-    grads[3][...] = product(left, value_grad[...]).astype(jnp.bfloat16).reshape(shape)
+    grads[1][...] = product(left, key_grad[...]).astype(jnp.bfloat16).reshape(shape)
+    grads[2][...] = product(left, value_grad[...]).astype(jnp.bfloat16).reshape(shape)
     summed.turn(1)
     for load in loads:
         load.wait()
@@ -997,55 +1104,44 @@
         return carry
 
     lax.fori_loop(0, total_rows // 256, weigh, 0)
-    first = lax.div(replica * hidden_share, tile)
-    last = lax.div((replica + 1) * hidden_share - 1, tile)
-
-    def each_tile(at, carry):
-        slot = lax.rem(at, 2)
-        for load in weight_loads(at, slot) + own_loads(at, slot):
-            load.wait()
-
-        @pl.when(at + 1 < tiles)
+    turn_tiles = (0, 2, 4, 6, 8, 10)
+    blocks = 1 if chunk <= 512 else 2
+
+    def each_tile(turn, carry):
+        slot = lax.rem(turn, 2)
+        at = tile_at(turn)
+        wait_all(weight_loads(at, slot) + own_loads(at, slot))
+
+        @pl.when(turn + 1 < tiles)
         def _():
-            for load in weight_loads(at + 1, 1 - slot) + own_loads(at + 1, 1 - slot):
-                load.start()
+            start_all(weight_loads(tile_at(turn + 1), 1 - slot) + own_loads(tile_at(turn + 1), 1 - slot))
 
         for number in range(2, summed.turns):
-            @pl.when(at == number - 2)
+            @pl.when(turn == turn_tiles[number - 2])
             def _(number=number):
                 summed.turn(number)
 
-        def each_block(block, carry):
-            cut = pl.ds(pl.multiple_of(block * slots, slots), slots)
+        @pl.when(turn >= 2)
+        def _():
+            wait_all(out_copies(tile_at(turn - 2), slot))
+
+        size = 2 * chunk // blocks
+        for block in range(blocks):
+            cut = pl.ds(ready + block * size, size)
             value, slope = gelu_parts(product(rows[cut, :width], mats[0, slot]))
             up_part = product(rows[cut, :width], mats[1, slot])
             back = product_back(cots[cut], own_mats[slot])
-            place = pl.ds(pl.multiple_of((block - 1) * slots, slots), slots)
-            tiles_of[0, place] = (value * up_part).astype(jnp.bfloat16)
-            tiles_of[1, place] = (back * up_part * slope).astype(jnp.bfloat16)
-            tiles_of[2, place] = (back * value).astype(jnp.bfloat16)
-            return carry
-
-        lax.fori_loop(1, total_rows // slots, each_block, 0)
-
-        @pl.when(at >= 2)
+            tiles_of[slot, 0, cut] = (value * up_part).astype(jnp.bfloat16)
+            tiles_of[slot, 1, cut] = (back * up_part * slope).astype(jnp.bfloat16)
+            tiles_of[slot, 2, cut] = (back * value).astype(jnp.bfloat16)
+        for number in range(2):
+            out_tiles[number, slot] = product(rows_left[...], tiles_of[slot, number + 1])
+        start_all(out_copies(at, slot))
+
+        @pl.when(turn < spans)
         def _():
-            for copy in out_copies(at - 2, slot):
-                copy.wait()
-
-        for number in range(2):
-            out_tiles[number, slot] = product(rows_left[:, :slots], own_tiles[number + 1, slot]) + product(
-                rows_left[:, slots:], tiles_of[number + 1]
-            )
-        for copy in out_copies(at, slot):
-            copy.start()
-
-        @pl.when((at >= first) & (at <= last))
-        def _():
-            place = pl.ds(pl.multiple_of((at - first) * tile, tile), tile)
-            down_tiles[place] = product_left(own_tiles[0, slot], cots[:slots]) + product_left(
-                tiles_of[0], cots[slots:]
-            )
+            place = pl.ds(pl.multiple_of(turn * tile, tile), tile)
+            down_tiles[place] = product_left(tiles_of[slot, 0], cots[...])
 
         return carry
 
@@ -1053,22 +1149,33 @@
     offset = pl.multiple_of(replica * hidden_share - first * tile, 8)
     down_copy = pltpu.make_async_copy(down_tiles.at[pl.ds(offset, hidden_share)], down_out, down_sem)
     down_copy.start()
-    for at in (tiles - 2, tiles - 1):
-        for copy in out_copies(at, at % 2):
-            copy.wait()
-    for number in range(tiles + 2, summed.turns):
-        summed.turn(number)
+    experts, room, capacity = slot_sizes
+    tok = normed.shape[0]
+    live = iota((tok, 1), 0) + lax.axis_index("erow") * tok < lengths[0]
+    slots = column_slots(columns_of(near_row[...], 2), live, experts, room, capacity)
+    names = iota((tok, experts * room), 1).astype(jnp.float32)
+    columns = columns_of(routes_true[...], 2)
+    lane = iota((tok, LANES), 1).astype(jnp.float32)
+    total = residual[...]
+    wait_all(returns)
+    results = out_landed[...].reshape(experts * room, width)
+    for k in range(2):
+        hot = jnp.where(names == slots[k], 1.0, 0.0).astype(jnp.bfloat16)
+        pick = jnp.sum(jnp.where(columns[:, k : k + 1] == lane, gates_in[...], 0.0), axis=1, keepdims=True)
+        total = total + pick * product(hot, results)
+    output[...] = total.astype(jnp.bfloat16)
+    for turn in (tiles - 2, tiles - 1):
+        wait_all(out_copies(tile_at(turn), turn % 2))
     down_copy.wait()
 
 
-def last(sizes, number, shared, small, rows_in, cots_in, own_in, weights):
+def last(sizes, number, slot_sizes, placing, shared, small, rows_in, cots_in, parts_in, out_sent, weights):
     n_dp, n_row, n_col = sizes
     normed = shared[0]
     tok, width = normed.shape
     hidden_width = weights[0].shape[1]
-    slots = own_in[0].shape[0]
-    total_rows = n_dp * slots
-    tile = 256
+    total_rows = sum(piece.shape[0] for piece in rows_in)
+    tile = parts_in.shape[3]
     depth = width // (n_dp * n_row * n_col)
     strip = n_col * depth
     half, single = jnp.bfloat16, jnp.float32
@@ -1077,44 +1184,85 @@
     hidden_share = hidden_width // n_dp
     spans = -(-hidden_share // tile) + 1
     scratch = [
+        pltpu.VMEM(out_sent.shape, half),
+        pltpu.SemaphoreType.DMA,
+        pltpu.SemaphoreType.DMA((n_row * n_col - 1,)),
+        pltpu.SemaphoreType.DMA((n_row * n_col - 1,)),
         pltpu.VMEM((total_rows, width + LANES), half),
         pltpu.VMEM((total_rows, width), half),
         pltpu.VMEM((width // n_dp, total_rows), half),
         pltpu.VMEM((2, 2, width, tile), half),
-        pltpu.VMEM((3, 2, slots, tile), half),
-        pltpu.VMEM((3, total_rows - slots, tile), half),
+        pltpu.VMEM((2, 3, total_rows, tile), half),
         pltpu.VMEM((2, tile, width), half),
         pltpu.VMEM((2, 2, width // n_dp, tile), single),
         pltpu.VMEM((spans * tile, width), single),
     ]
-    scratch += [pltpu.VMEM((2, 2, n_row, strip, width), half)] * 4
-    for _ in range(4):
+    scratch += [pltpu.VMEM((2, 2, n_row, strip, width), half)] * 3
+    for _ in range(3):
         scratch += share_scratch((n_row, n_col), depth, width, half)
     scratch += share_scratch((n_row, n_col), depth, LANES, single)
-    sems = (5, 4 + n_col)
+    sems = (4, 4 + n_col)
     scratch += [
-        pltpu.SemaphoreType.DMA((2, 5)),
+        pltpu.SemaphoreType.DMA((2, len(rows_in))),
         pltpu.SemaphoreType.DMA((3, 2)),
-        pltpu.SemaphoreType.DMA((3, 2)),
+        pltpu.SemaphoreType.DMA((2,)),
         pltpu.SemaphoreType.DMA((2, 2)),
         pltpu.SemaphoreType.DMA,
         pltpu.SemaphoreType.DMA(sems),
         pltpu.SemaphoreType.DMA(sems),
     ]
-    out_shape = [jax.ShapeDtypeStruct((depth, width), single)] * 4
+    out_shape = [jax.ShapeDtypeStruct((depth, width), single)] * 3
     out_shape += [jax.ShapeDtypeStruct((depth, LANES), single)]
     out_shape += [jax.ShapeDtypeStruct((width // n_dp, hidden_width), single)] * 2
-    out_shape += [jax.ShapeDtypeStruct((hidden_share, width), single)]
+    out_shape += [jax.ShapeDtypeStruct((hidden_share, width), single), jax.ShapeDtypeStruct((tok, width), half)]
     return pl.pallas_call(
-        functools.partial(last_kernel, tile, (n_row, n_col), depth),
+        functools.partial(last_kernel, tile, (n_row, n_col), depth, slot_sizes),
         out_shape=out_shape,
-        in_specs=[vmem] * 7 + [anywhere] * 16,
-        out_specs=[vmem] * 5 + [anywhere] * 3,
+        in_specs=[pl.BlockSpec(memory_space=pltpu.SMEM)] + [vmem] * 9 + [anywhere] * (2 * len(rows_in) + 5),
+        out_specs=[vmem] * 4 + [anywhere] * 3 + [vmem],
         scratch_shapes=scratch,
         compiler_params=pltpu.CompilerParams(
             collective_id=number, has_side_effects=True, vmem_limit_bytes=VMEM_LIMIT
         ),
-    )(*shared, small, *rows_in, *cots_in, *own_in, *weights)
+    )(*placing, *shared, small, *rows_in, *cots_in, parts_in, out_sent, *weights)
+
+
+def finish_kernel(experts, bias_share, small, *refs):
+    count = (len(refs) - 5) // 3
+    sources, targets, rest = refs[:count], refs[count : 2 * count], refs[2 * count :]
+    (attn_out, moe_out, bias_out, router_out), held, sems = rest[:4], rest[4:-1], rest[-1]
+    loads = [
+        pltpu.make_async_copy(source, place, sems.at[0, at]) for at, (source, place) in enumerate(zip(sources, held))
+    ]
+    stores = [
+        pltpu.make_async_copy(place, target, sems.at[1, at]) for at, (place, target) in enumerate(zip(held, targets))
+    ]
+    start_all(loads)
+    turned = small[...].T
+    attn_out[...] = turned[LANES - 3 : LANES - 2]
+    moe_out[...] = turned[LANES - 2 : LANES - 1]
+    bias_out[...] = turned[LANES - 1 :, :bias_share]
+    router_out[...] = turned[:experts]
+    for load, store in zip(loads, stores):
+        load.wait()
+        store.start()
+    wait_all(stores)
+
+
+def finish(experts, bias_share, small, *arrays):
+    depth = small.shape[0]
+    vmem, anywhere = pl.BlockSpec(memory_space=pltpu.VMEM), pl.BlockSpec(memory_space=pl.ANY)
+    shapes = [(array.shape, array.dtype) for array in arrays]
+    shapes += [((1, depth), small.dtype)] * 2 + [((1, bias_share), small.dtype), ((experts, depth), small.dtype)]
+    return pl.pallas_call(
+        functools.partial(finish_kernel, experts, bias_share),
+        out_shape=[jax.ShapeDtypeStruct(*shape) for shape in shapes],
+        in_specs=[vmem] + [anywhere] * len(arrays),
+        out_specs=[anywhere] * len(arrays) + [vmem] * 4,
+        scratch_shapes=[pltpu.VMEM(array.shape, array.dtype) for array in arrays]
+        + [pltpu.SemaphoreType.DMA((2, len(arrays)))],
+        compiler_params=pltpu.CompilerParams(vmem_limit_bytes=VMEM_LIMIT),
+    )(small, *arrays)
 
 
 def gelu_parts(gate_part):
@@ -1126,8 +1274,11 @@
     return value, slope
 
 
-def flat(*pieces):
-    return [piece.reshape(-1, piece.shape[-1]) for piece in pieces]
+def paired(own, *pieces):
+    blocks = [own]
+    for at in range(0, len(pieces), 2):
+        blocks += [pieces[at][0], pieces[at + 1][0], pieces[at][1], pieces[at + 1][1]]
+    return [block.reshape(-1, block.shape[-1]) for block in blocks]
 
 
 def body(
@@ -1156,19 +1307,20 @@
     device_count = n_dp * n_row * n_col
     slot_count = expert_count * room
     gate_mat, up_mat, down_mat = gate_weight[0], up_weight[0], down_weight[0]
-    near_routes = ((routes[0] % n_col) ^ lax.axis_index("ecol")) * n_row + (
-        (routes[0] // n_col) ^ lax.axis_index("erow")
-    )
-    router = jnp.pad(router_weight, ((0, 0), (0, LANES - expert_count)))
+    routes_row = routes[0].T
+    near_routes = mirrored((routes_row % n_col) ^ lax.axis_index("ecol"), n_col) * n_row + (
+        (routes_row // n_col) ^ lax.axis_index("erow")
+    )
+    router = router_weight.T
     dims = (head_count, expert_count, room, capacity, n_row, n_col)
-    normed, queries, both, probs, mixed, residual, gates, slot_rows, got_grads, near_grads = front(
+    normed, queries, both, probs, mixed, residual, gates, slot_rows, got_grads, *cots0 = front(
         dims,
         0,
         lengths,
         tokens[0],
         cotangent[0],
-        near_routes.T,
-        routes[0],
+        near_routes,
+        routes_row,
         attn_gain[None],
         moe_gain[None],
         relative_bias,
@@ -1178,29 +1330,20 @@
         value_weight,
         out_weight,
     )
-    (
-        back,
-        got,
-        expert_out,
-        own_hidden,
-        own_gate_back,
-        own_up_back,
-        far_grads,
-        near_grads_late,
-        far_grads_late,
-        near_rows,
-        far_rows,
-    ) = experts_apply((n_row, n_col), 1, slot_rows, got_grads, near_grads, gate_mat, up_mat, down_mat)
+    back, got, expert_out, parts, *moved = experts_apply(
+        (n_row, n_col), 1, 256 if slot_count <= 768 else LANES, slot_rows, got_grads, *cots0, gate_mat, up_mat, down_mat
+    )
+    cots1, cots2, cots3, rows0, rows1 = (moved[at : at + 2] for at in range(0, 10, 2))
     depth = width // device_count
     bias_share = head_count * bucket_count // device_count
-    output, token_grad, branch_grad, query_grad, key_grad, value_grad, small, near_rows_late, far_rows_late = backward(
+    token_grad, query_grad, key_grad, value_grad, small, *moved, out_sum = backward(
         dims + (bias_share, depth),
         2,
         lengths,
         tokens[0],
         cotangent[0],
         near_routes,
-        routes[0],
+        routes_row,
         attn_gain[None],
         moe_gain[None],
         router,
@@ -1211,34 +1354,53 @@
         queries,
         both,
         back,
-        expert_out,
         got,
         query_weight,
         key_weight,
         value_weight,
         out_weight,
     )
-    out_sum, query_sum, key_sum, value_sum, small_sum, gate_total, up_total, down_total = last(
+    rows2, rows3 = moved[:2], moved[2:]
+    query_sum, key_sum, value_sum, small_sum, gate_total, up_total, down_total, output = last(
         (n_dp, n_row, n_col),
         3,
-        (normed, query_grad, key_grad, value_grad, mixed, branch_grad),
+        (expert_count, room, capacity),
+        (lengths, near_routes, routes_row, residual, gates),
+        (normed, query_grad, key_grad, value_grad),
         small,
-        flat(got, near_rows, far_rows, near_rows_late, far_rows_late),
-        flat(got_grads, near_grads, far_grads, near_grads_late, far_grads_late),
-        (own_hidden, own_gate_back, own_up_back),
+        paired(got, rows0, rows1, rows2, rows3),
+        paired(got_grads, cots0, cots1, cots2, cots3),
+        parts,
+        expert_out,
         (gate_mat, up_mat, down_mat),
     )
-    return (
-        output[None],
-        token_grad[None],
-        small_sum[:, LANES - 3],
+    handed = finish(
+        expert_count,
+        bias_share,
+        small_sum,
+        output,
+        token_grad,
         query_sum,
         key_sum,
         value_sum,
         out_sum,
-        small_sum[:bias_share, LANES - 1],
-        small_sum[:, LANES - 2],
-        small_sum[:, :expert_count],
+        gate_total,
+        up_total,
+        down_total,
+    )
+    output, token_grad, query_sum, key_sum, value_sum, out_sum, gate_total, up_total, down_total = handed[:9]
+    attn_sum, moe_sum, bias_sum, router_sum = handed[9:]
+    return (
+        output[None],
+        token_grad[None],
+        attn_sum[0],
+        query_sum,
+        key_sum,
+        value_sum,
+        out_sum,
+        bias_sum[0],
+        moe_sum[0],
+        router_sum.T,
         gate_total[None],
         up_total[None],
         down_total[None],

time: 280 us -> 254 us (0.907); the launches traced: 275 us -> 254 us
  local copies, waits for them, and re-layouts: 19.3 us -> 0 us
    pallas_call x1 -> x2, Pallas kernels: 77.6 us -> 101 us  [the longest x1 91.1 us: experts_apply(): pl.pallas_call(functools.partial(expert_kernel, tile, sizes), out_shape=[...]
    pallas_call x1, Pallas kernels: 89.2 us -> 67.3 us  [last(): pl.pallas_call(functools.partial(last_kernel, tile, (n_row, n_col), depth...]
    unnamed x32 -> x0, local copies, waits for them, and re-layouts: 14.8 us -> none
    pallas_call x1, Pallas kernels: 43.8 us -> 34.2 us  [front(): pl.pallas_call(functools.partial(front_kernel, dims), out_shape=[jax.Shap...]
    pallas_call x1, Pallas kernels: 42.8 us -> 48.7 us  [backward(): pl.pallas_call(functools.partial(back_kernel, dims), out_shape=[jax.Shape...]
    slice x2 -> x0, local copies, waits for them, and re-layouts: 2.94 us -> none  [the longest x1 1.49 us: body(): small_sum[:, LANES - 2]]
where the time goes in v1:
time: 254 us
  Pallas kernels  251 us (99%)
    pallas_call x1, Pallas kernels, experts_apply(): pl.pallas_call(functools.partial(expert_kernel, tile, sizes), out_shape=[...  91.1 us
    pallas_call x1, Pallas kernels, last(): pl.pallas_call(functools.partial(last_kernel, tile, (n_row, n_col), depth...  67.3 us
    pallas_call x1, Pallas kernels, backward(): pl.pallas_call(functools.partial(back_kernel, dims), out_shape=[jax.Shape...  48.7 us
    pallas_call x1, Pallas kernels, front(): pl.pallas_call(functools.partial(front_kernel, dims), out_shape=[jax.Shap...  34.2 us
    pallas_call x1, Pallas kernels, finish(): pl.pallas_call(functools.partial(finish_kernel, experts, bias_share), out...  9.62 us

profile of v1, /device:TPU:0, one launch (start us, length us, event | category | flops | bytes accessed | tf_op | source)
XLA Modules:
  0.0 253.6 jit_solution(9235122388545424041)
XLA Ops:
  1.3 1.3 xor_add_fusion.routes_row.near_row.refs_1_
  2.6 34.2 %shard_map.246 = (bf16[256,1024]{1,0:T(8,128)(2,1)}, bf16[256,1024]{1,0:T(8,128)(2,1)}, bf16[512,2048]{1,0:T(8,128)(2,1)}, bf16[16,256,512]{2,1,0:T(8,128)(2,1)}...) custom-call(s32[1]{0:T(128)S(6)} %copy.28.lengths.refs_0_, ...), custom_call_target="tpu_custom_call" | custom-call | tf_op jit(solution)/shard_map/pallas_call | solution.py:439
  36.8 91.1 %shard_map.247 = (bf16[8,80,1152]{2,1,0:T(8,128)(2,1)}, bf16[8,80,1152]{2,1,0:T(8,128)(2,1)}, bf16[8,80,1024]{2,1,0:T(8,128)(2,1)}, bf16[11,3,1600,256]{3,2,1,0:...) custom-call(bf16[8,80,1152]{2,1,0:T(8,128)(2,1)} %get-tuple-element., ...), custom_call_target="tpu_custom_call" | custom-call | tf_op jit(solution)/shard_map/pallas_call | solution.py:702
  127.9 48.7 %shard_map.248 = (f32[256,1024]{1,0:T(8,128)}, bf16[256,1024]{1,0:T(8,128)(2,1)}, bf16[256,1024]{1,0:T(8,128)(2,1)}, bf16[256,1024]{1,0:T(8,128)(2,1)}, f32[1024...) custom-call(s32[1]{0:T(128)S(6)} %copy.28.lengths.refs_0_, ...), custom_call_target="tpu_custom_call" | custom-call | tf_op jit(solution)/shard_map/pallas_call | solution.py:990
  176.6 67.3 %shard_map.249 = (f32[32,1024]{1,0:T(8,128)}, f32[32,1024]{1,0:T(8,128)}, f32[32,1024]{1,0:T(8,128)}, f32[32,128]{1,0:T(8,128)}, f32[256,2816]{1,0:T(8,128)}, /*...) custom-call(s32[1]{0:T(128)S(6)} %copy.28.lengths.refs_0_, ...), custom_call_target="tpu_custom_call" | custom-call | tf_op jit(solution)/shard_map/pallas_call | solution.py:1218
  243.8 9.6 %shard_map.250 = (bf16[256,1024]{1,0:T(8,128)(2,1)}, f32[256,1024]{1,0:T(8,128)}, f32[32,1024]{1,0:T(8,128)}, f32[32,1024]{1,0:T(8,128)}, f32[32,1024]{1,0:T(8,1...) custom-call(f32[32,128]{1,0:T(8,128)} %get-tuple-element.102.small, ...), custom_call_target="tpu_custom_call" | custom-call | tf_op jit(solution)/shard_map/pallas_call | solution.py:1257

commit v2 on v1

--- a/solution.py
+++ b/solution.py
@@ -283,8 +283,9 @@
     gates_out,
     rows_out,
     cot_landed,
-    cot_near,
-    cot_far,
+    cot_near0,
+    cot_far0,
+    cot_near1,
     select,
     cot_slots,
     tables,
@@ -307,10 +308,13 @@
         load.start()
         loads.append(load)
     devices = partners(n_row, n_col)
-    spread = Spread(cot_near, cot_far, near_send, near_recv)
+    spreads = [
+        Spread(near, far, near_send.at[at], near_recv.at[at])
+        for at, (near, far) in enumerate(((cot_near0, cot_far0), (cot_near1, None)))
+    ]
     part = len(devices) // 4
     barrier = pltpu.get_barrier_semaphore()
-    for device in devices[1:] + spread.devices:
+    for device in devices[1:] + spreads[0].devices:
         pl.semaphore_signal(barrier, 1, device_id=device, device_id_type=MESH)
 
     piece = lax.axis_index("erow")
@@ -323,18 +327,20 @@
     cot_slots[...] = product(select[...], cotangent[...]).astype(jnp.bfloat16).reshape(cot_slots.shape)
     pl.semaphore_wait(barrier, len(devices) + 1)
     own = pltpu.make_async_copy(cot_slots.at[0], cot_landed.at[0], own_sem)
-    own.start()
-    copies = []
-    for place in range(1, len(devices)):
-        copy = remote(
+    copies = [own] + [
+        remote(
             cot_slots.at[place],
             cot_landed.at[place],
             send_sems.at[place - 1],
             recv_sems.at[place - 1],
             devices[place],
         )
-        copy.start()
-        copies.append(copy)
+        for place in range(1, len(devices))
+    ]
+    start_all(copies)
+
+    def cots_first(piece):
+        return spreads[piece].first(cot_landed.at[pl.ds(piece * part, part)])
 
     inputs = tokens[...].astype(jnp.float32)
     scale = lax.rsqrt(jnp.mean(inputs * inputs, axis=1, keepdims=True) + epsilon)
@@ -364,13 +370,13 @@
 
         @pl.when(pair == 0)
         def _():
-            wait_all([own] + copies[: part - 1])
-            start_all(spread.first(cot_landed.at[pl.ds(0, part)]))
+            wait_all(copies[:part])
+            start_all(cots_first(0))
 
         @pl.when(pair == heads // 4)
         def _():
-            wait_all(spread.first(cot_landed.at[pl.ds(0, part)]))
-            start_all(spread.second())
+            wait_all(cots_first(0))
+            start_all(spreads[0].second())
 
         results = []
         for member in range(2):
@@ -388,6 +394,8 @@
         return carry
 
     lax.fori_loop(0, heads // 2, attend, 0)
+    wait_all(copies[part : 2 * part])
+    start_all(cots_first(1))
     loads[3].wait()
     residual = inputs + product(mixed_out[...], held_weights[3])
     residual_out[...] = residual
@@ -412,8 +420,8 @@
     rows = product(select[...], moe_in.astype(jnp.bfloat16))
     rows_out[:, :, :width] = rows.astype(jnp.bfloat16).reshape(rows_out.shape[0], -1, width)
     rows_out[:, :, width:] = panel.astype(jnp.bfloat16).reshape(rows_out.shape[0], -1, LANES)
-    wait_all(copies[part - 1 :])
-    wait_all(spread.second())
+    wait_all(copies[2 * part :])
+    wait_all(spreads[0].second() + cots_first(1))
 
 
 def front(dims, number, lengths, tokens, cotangent, routes_row, routes_col, *params):
@@ -436,11 +444,12 @@
         ((2, group // 4, blocks, width), half),
         ((group // 4, blocks, width), half),
     ]
+    shapes += shapes[-2:-1]
     return pl.pallas_call(
         functools.partial(front_kernel, dims),
         out_shape=[jax.ShapeDtypeStruct(shape, kind) for shape, kind in shapes],
         in_specs=[pl.BlockSpec(memory_space=pltpu.SMEM)] + [vmem] * 8 + [anywhere] * 4,
-        out_specs=[vmem] * 8 + [anywhere] * 3,
+        out_specs=[vmem] * 8 + [anywhere] * 4,
         scratch_shapes=[
             pltpu.VMEM((experts * room, tok), half),
             pltpu.VMEM((group, blocks, width), half),
@@ -452,8 +461,8 @@
             pltpu.SemaphoreType.DMA((group - 1,)),
             pltpu.SemaphoreType.DMA,
             pltpu.SemaphoreType.DMA,
-            pltpu.SemaphoreType.DMA((4,)),
-            pltpu.SemaphoreType.DMA((4,)),
+            pltpu.SemaphoreType.DMA((2, 4)),
+            pltpu.SemaphoreType.DMA((2, 4)),
         ],
         compiler_params=pltpu.CompilerParams(
             collective_id=number, has_side_effects=True, vmem_limit_bytes=VMEM_LIMIT
@@ -472,6 +481,7 @@
     cot_own,
     cot_near0,
     cot_far0,
+    cot_near1,
     gate_weight,
     up_weight,
     down_weight,
@@ -479,7 +489,6 @@
     rows_landed,
     out_rows,
     parts_out,
-    cot_near1,
     cot_far1,
     cot_near2,
     cot_far2,
@@ -489,6 +498,8 @@
     rows_far0,
     rows_near1,
     rows_far1,
+    rows_near2,
+    rows_far2,
     gate_mat,
     up_mat,
     down_mat,
@@ -529,7 +540,9 @@
     ]
     row_spreads = [
         Spread(near, far, spread_send.at[3 + at], spread_recv.at[3 + at])
-        for at, (near, far) in enumerate(((rows_near0, rows_far0), (rows_near1, rows_far1)))
+        for at, (near, far) in enumerate(
+            ((rows_near0, rows_far0), (rows_near1, rows_far1), (rows_near2, rows_far2))
+        )
     ]
     greet(devices[1:] + row_spreads[0].devices)
 
@@ -605,6 +618,10 @@
         start_all([row_copy(1, place) for place in range(half * part, (half + 1) * part)])
         stage_end(half * strip, strip)
 
+    def late_seconds():
+        wait_all(cots_first(2) + cots_first(3) + rows_first(2))
+        start_all(cot_spreads[2].second() + cot_spreads[3].second() + row_spreads[2].second())
+
     def others(start, sources):
         at, copies = 0, []
         for number, (row_source, cot_source) in enumerate(sources):
@@ -624,6 +641,7 @@
         size = size * room
 
         def middle(at, carry):
+            pl.when(at == tiles // 2)(late_seconds)
             stage_free(at, start, size)
             cut = pl.ds(pl.multiple_of(at * tile, tile), tile)
             value, slope = gelu_parts(product(rows, gate_mat[:, cut]))
@@ -644,7 +662,7 @@
         stage_end(start, size)
 
     start_all([row_copy(0, place) for place in range(part)])
-    start_all(cots_first(1))
+    start_all(cot_spreads[1].second() + cots_first(2))
     wait_all(loads[:2])
     cot_rows = cot[...].reshape(group * room, width)
 
@@ -661,19 +679,17 @@
     start_all([row_copy(0, place) for place in range(part, group)])
     start_all(rows_first(1))
     own_half(0)
-    wait_all(cots_first(1) + rows_first(0))
-    start_all(cot_spreads[1].second() + row_spreads[0].second() + cots_first(2))
-    others(2 * strip, [(rows_near0.at[k], cot_near0.at[k]) for k in range(2)])
-    wait_all(rows_first(1))
-    start_all(row_spreads[1].second() + cots_first(3))
+    wait_all(rows_first(0) + rows_first(1))
+    start_all(row_spreads[0].second() + row_spreads[1].second() + cots_first(3))
     wait_all([row_copy(0, place) for place in range(part, group)])
+    start_all(rows_first(2))
     own_half(1)
-    wait_all(cots_first(2) + cots_first(3))
-    start_all(cot_spreads[2].second() + cot_spreads[3].second())
     wait_all(cot_spreads[1].second() + row_spreads[0].second() + row_spreads[1].second())
     others(
-        3 * strip,
-        [(rows_near1.at[k], cot_near1.at[k]) for k in range(2)] + [(rows_far0, cot_far0), (rows_far1, cot_far1)],
+        2 * strip,
+        [(rows_near0.at[k], cot_near0.at[k]) for k in range(2)]
+        + [(rows_near1.at[k], cot_near1.at[k]) for k in range(2)]
+        + [(rows_far0, cot_far0), (rows_far1, cot_far1)],
     )
 
     def outward(at, carry):
@@ -684,26 +700,26 @@
 
     lax.fori_loop(0, width // tile, outward, 0)
     wait_all([row_copy(1, place) for place in range(group)])
-    wait_all(cot_spreads[2].second() + cot_spreads[3].second())
+    wait_all(cot_spreads[2].second() + cot_spreads[3].second() + row_spreads[2].second())
 
 
 def experts_apply(sizes, number, tile, *operands):
     rows_sent, cot_own = operands[:2]
     group, room, width = cot_own.shape
-    hidden_width = operands[4].shape[1]
+    hidden_width = operands[5].shape[1]
     slots = group * room
     quarter = group // 4
     half, single = jnp.bfloat16, jnp.float32
     vmem, anywhere = pl.BlockSpec(memory_space=pltpu.VMEM), pl.BlockSpec(memory_space=pl.ANY)
     wide = rows_sent.shape[2]
     shapes = [rows_sent.shape, rows_sent.shape, cot_own.shape, (hidden_width // tile, 3, 5 * slots // 2, tile)]
-    shapes += [(2, quarter, room, width), (quarter, room, width)] * 3
-    shapes += [(2, quarter, room, wide), (quarter, room, wide)] * 2
+    shapes += [(quarter, room, width)] + [(2, quarter, room, width), (quarter, room, width)] * 2
+    shapes += [(2, quarter, room, wide), (quarter, room, wide)] * 3
     return pl.pallas_call(
         functools.partial(expert_kernel, tile, sizes),
         out_shape=[jax.ShapeDtypeStruct(shape, half) for shape in shapes],
-        in_specs=[anywhere] * 7,
-        out_specs=[anywhere] + [vmem] * 2 + [anywhere] * 11,
+        in_specs=[anywhere] * 8,
+        out_specs=[anywhere] + [vmem] * 2 + [anywhere] * 12,
         scratch_shapes=[
             pltpu.VMEM((width, hidden_width), half),
             pltpu.VMEM((width, hidden_width), half),
@@ -714,17 +730,17 @@
             pltpu.VMEM((slots // 2, width), single),
             pltpu.VMEM((slots // 2, LANES), single),
             pltpu.VMEM(rows_sent.shape, half),
-            pltpu.VMEM((4 * quarter, room, wide), half),
-            pltpu.VMEM((4 * quarter, room, width), half),
-            pltpu.VMEM((2, 3, slots, tile), half),
+            pltpu.VMEM((6 * quarter, room, wide), half),
+            pltpu.VMEM((6 * quarter, room, width), half),
+            pltpu.VMEM((2, 3, 6 * quarter * room, tile), half),
             pltpu.SemaphoreType.DMA((4,)),
             pltpu.SemaphoreType.DMA((2,)),
             pltpu.SemaphoreType.DMA((2, group - 1)),
             pltpu.SemaphoreType.DMA((2, group - 1)),
-            pltpu.SemaphoreType.DMA((5, 4)),
-            pltpu.SemaphoreType.DMA((5, 4)),
+            pltpu.SemaphoreType.DMA((6, 4)),
+            pltpu.SemaphoreType.DMA((6, 4)),
             pltpu.SemaphoreType.DMA((2,)),
-            pltpu.SemaphoreType.DMA((2, 4)),
+            pltpu.SemaphoreType.DMA((2, 6)),
         ],
         compiler_params=pltpu.CompilerParams(
             collective_id=number, has_side_effects=True, vmem_limit_bytes=VMEM_LIMIT
@@ -768,23 +784,26 @@
     probs_in,
     queries_in,
     both,
+    normed,
     back_in,
+    out_sent,
     rows_own,
     query_weight,
     key_weight,
     value_weight,
     out_weight,
+    output,
     token_grad,
-    query_grad,
-    key_grad,
-    value_grad,
+    query_wgrad,
+    key_wgrad,
+    value_wgrad,
     small,
-    rows_near2,
-    rows_far2,
     rows_near3,
     rows_far3,
     out_total,
     back,
+    out_landed,
+    query_grad,
     held_weights,
     mixed_back,
     residual_grad,
@@ -793,6 +812,9 @@
     near_sum,
     diagonals,
     load_sems,
+    own_sem,
+    send_sems,
+    recv_sems,
     row_send,
     row_recv,
     near_send,
@@ -815,18 +837,18 @@
         load.start()
         loads.append(load)
     devices = partners(n_row, n_col)
-    spreads = [
-        Spread(near, far, near_send.at[at], near_recv.at[at])
-        for at, (near, far) in enumerate(((rows_near2, rows_far2), (rows_near3, rows_far3)))
-    ]
+    spread = Spread(rows_near3, rows_far3, near_send, near_recv)
     quarter = len(devices) // 4
+    late_rows = rows_own.at[pl.ds(3 * quarter, quarter)]
     summed = ShareSum((n_row, n_col), depth, [out_wgrad], [out_total], [held], sum_send, sum_recv)
-    greet(devices[1:] + spreads[0].devices)
-
-    def rows_first(at):
-        return spreads[at].first(rows_own.at[pl.ds((2 + at) * quarter, quarter)])
-
-    start_all(rows_first(0))
+    greet(devices[1:] + spread.devices)
+    start_all(spread.first(late_rows))
+    copies = [pltpu.make_async_copy(out_sent.at[0], out_landed.at[0], own_sem)]
+    for place in range(1, len(devices)):
+        sems = (send_sems.at[place - 1], recv_sems.at[place - 1])
+        copies.append(remote(out_sent.at[place], out_landed.at[place], *sems, devices[place]))
+    start_all(copies)
+
     piece = lax.axis_index("erow")
     live = iota((tok, 1), 0) + piece * tok < lengths[0]
     slots = column_slots(columns_of(near_row[...], 2), live, experts, room, capacity)
@@ -886,8 +908,8 @@
 
         @pl.when(pair == 3)
         def _():
-            wait_all(rows_first(0))
-            start_all(spreads[0].second() + rows_first(1))
+            wait_all(spread.first(late_rows))
+            start_all(spread.second())
 
         @pl.when(pair == 5)
         def _():
@@ -928,6 +950,9 @@
     lax.fori_loop(0, heads // 2, unattend, 0)
     pair_copy = remote(far_sent, far_landed, row_send, row_recv, devices[1])
     pair_copy.start()
+    left = normed[...].T
+    shape = query_wgrad.shape
+    query_wgrad[...] = product(left, query_grad[...]).astype(jnp.bfloat16).reshape(shape)
 
     segment = width // heads
     table = 4 * tok
@@ -954,10 +979,8 @@
     pair_copy.wait()
     key_total = (near_sum[:, :width] + far_landed[:, :width].astype(jnp.float32)).astype(jnp.bfloat16)
     value_total = (near_sum[:, width:] + far_landed[:, width:].astype(jnp.float32)).astype(jnp.bfloat16)
-    wait_all(rows_first(1))
-    start_all(spreads[1].second())
-    key_grad[...] = key_total
-    value_grad[...] = value_total
+    key_wgrad[...] = product(left, key_total).astype(jnp.bfloat16).reshape(shape)
+    value_wgrad[...] = product(left, value_total).astype(jnp.bfloat16).reshape(shape)
     loads[3].wait()
     loads[4].wait()
     normed_back = normed_back + product_back(key_total, held_weights[2]) + product_back(value_total, held_weights[3])
@@ -972,28 +995,38 @@
     )
     empty = jnp.zeros((LANES - 3, width), jnp.float32)
     small[...] = jnp.concatenate([empty, attn_gain_grad, moe_gain_grad, bias_row], axis=0).T + router_grad
-    wait_all(spreads[0].second() + spreads[1].second())
+    wait_all(copies)
+    results = out_landed[...].reshape(slots_count, width)
+    total = residual
+    for k in range(2):
+        pick = jnp.sum(jnp.where(chosen[k], gates, 0.0), axis=1, keepdims=True)
+        total = total + pick * product(hot[k], results)
+    output[...] = total.astype(jnp.bfloat16)
+    wait_all(spread.second())
     summed.turn(4)
 
 
 def backward(dims, number, *operands):
     heads, experts, room, capacity, n_row, n_col, share, depth = dims
-    tokens, back_in, rows_own = operands[1], operands[14], operands[15]
+    tokens, back_in, out_sent, rows_own = operands[1], operands[15], operands[16], operands[17]
     tok, width = tokens.shape
     group = n_row * n_col
     half, single = jnp.bfloat16, jnp.float32
     vmem, anywhere = pl.BlockSpec(memory_space=pltpu.VMEM), pl.BlockSpec(memory_space=pl.ANY)
-    shapes = [((tok, width), single)] + [((tok, width), half)] * 3 + [((width, LANES), single)]
-    shapes += [((2, group // 4) + rows_own.shape[1:], half), ((group // 4,) + rows_own.shape[1:], half)] * 2
+    wgrad = (2, 2, n_row, n_col * depth, width)
+    shapes = [((tok, width), half), ((tok, width), single)] + [(wgrad, half)] * 3 + [((width, LANES), single)]
+    shapes += [((2, group // 4) + rows_own.shape[1:], half), ((group // 4,) + rows_own.shape[1:], half)]
     shapes += [((depth, width), single)]
     sems = (1, 4 + n_col)
     return pl.pallas_call(
         functools.partial(back_kernel, dims),
         out_shape=[jax.ShapeDtypeStruct(shape, kind) for shape, kind in shapes],
-        in_specs=[pl.BlockSpec(memory_space=pltpu.SMEM)] + [vmem] * 13 + [anywhere] * 6,
-        out_specs=[vmem] * 5 + [anywhere] * 4 + [vmem],
+        in_specs=[pl.BlockSpec(memory_space=pltpu.SMEM)] + [vmem] * 14 + [anywhere] * 7,
+        out_specs=[vmem] * 6 + [anywhere] * 2 + [vmem],
         scratch_shapes=[
             pltpu.VMEM(back_in.shape, half),
+            pltpu.VMEM(out_sent.shape, half),
+            pltpu.VMEM((tok, width), half),
             pltpu.VMEM((4, width, width), half),
             pltpu.VMEM((tok, width), half),
             pltpu.VMEM((tok, width), single),
@@ -1003,10 +1036,13 @@
             pltpu.VMEM((heads, 4 * tok), single),
             pltpu.SemaphoreType.DMA((5,)),
             pltpu.SemaphoreType.DMA,
+            pltpu.SemaphoreType.DMA((group - 1,)),
+            pltpu.SemaphoreType.DMA((group - 1,)),
             pltpu.SemaphoreType.DMA,
-            pltpu.SemaphoreType.DMA((2, 4)),
-            pltpu.SemaphoreType.DMA((2, 4)),
-            pltpu.VMEM((2, 2, n_row, n_col * depth, width), half),
+            pltpu.SemaphoreType.DMA,
+            pltpu.SemaphoreType.DMA((4,)),
+            pltpu.SemaphoreType.DMA((4,)),
+            pltpu.VMEM(wgrad, half),
         ]
         + share_scratch((n_row, n_col), depth, width, half)
         + [pltpu.SemaphoreType.DMA(sems), pltpu.SemaphoreType.DMA(sems)],
@@ -1016,20 +1052,17 @@
     )(*operands)
 
 
-def last_kernel(tile, sizes, depth, slot_sizes, *refs):
+def last_kernel(tile, sizes, depth, *refs):
     pieces = 9
-    (lengths, near_row, routes_true, residual, gates_in), refs = refs[:5], refs[5:]
-    (normed, query_grad, key_grad, value_grad, small), refs = refs[:5], refs[5:]
+    grads, small, refs = refs[:3], refs[3], refs[4:]
     rows_in, refs = refs[:pieces], refs[pieces:]
     cots_in, refs = refs[:pieces], refs[pieces:]
-    parts_in, out_sent, weights, sums, refs = refs[0], refs[1], refs[2:5], refs[5:9], refs[9:]
-    (gate_out, up_out, down_out, output), refs = refs[:4], refs[4:]
-    (out_landed, out_own, out_send, out_recv), refs = refs[:4], refs[4:]
-    (rows, cots, rows_left, mats, tiles_of, own_mats, out_tiles, down_tiles), refs = refs[:8], refs[8:]
-    grads, refs = refs[:3], refs[3:]
+    parts_in, weights, sums, refs = refs[0], refs[1:4], refs[4:8], refs[8:]
+    (gate_out, up_out, down_out), refs = refs[:3], refs[3:]
+    (rows, cots, mats, tiles_of, own_mats, out_tiles, down_tiles), refs = refs[:7], refs[7:]
     held, refs = [refs[5 * at : 5 * at + 5] for at in range(4)], refs[20:]
     load_sems, weight_sems, own_sems, out_sems, down_sem, send_sems, recv_sems = refs
-    width, strip = normed.shape[1], grads[0].shape[3]
+    width = grads[0].shape[4]
     hidden_width = weights[0].shape[1]
     tiles = hidden_width // tile
     ready = parts_in.shape[2]
@@ -1040,8 +1073,7 @@
     replica = lax.axis_index("dp")
     summed = ShareSum(sizes, depth, list(grads) + [small], sums, held, send_sems, recv_sems)
     barrier = pltpu.get_barrier_semaphore()
-    devices = partners(*sizes)
-    for device in devices[1:] + summed.devices[1:3]:
+    for device in summed.devices:
         pl.semaphore_signal(barrier, 1, device_id=device, device_id_type=MESH)
     loads, start = [], 0
     for at, (row_piece, cot_piece) in enumerate(zip(rows_in, cots_in)):
@@ -1071,6 +1103,7 @@
             for number, target in enumerate((gate_out, up_out))
         ]
 
+    share_lanes = pl.ds(pl.multiple_of(replica * share, share), share)
     first = lax.div(replica * hidden_share, tile)
     spans = lax.div((replica + 1) * hidden_share - 1, tile) - first + 1
 
@@ -1078,19 +1111,8 @@
         return lax.rem(first + turn, tiles)
 
     start_all(weight_loads(tile_at(0), 0) + own_loads(tile_at(0), 0))
-    left = normed[...].T
-    shape = grads[0].shape
-    grads[0][...] = product(left, query_grad[...]).astype(jnp.bfloat16).reshape(shape)
-    pl.semaphore_wait(barrier, len(devices) + 1)
-    returns = [pltpu.make_async_copy(out_sent.at[0], out_landed.at[0], out_own)]
-    for place in range(1, len(devices)):
-        sems = (out_send.at[place - 1], out_recv.at[place - 1])
-        returns.append(remote(out_sent.at[place], out_landed.at[place], *sems, devices[place]))
-    start_all(returns)
+    pl.semaphore_wait(barrier, len(summed.devices))
     summed.turn(0)
-    grads[1][...] = product(left, key_grad[...]).astype(jnp.bfloat16).reshape(shape)
-    grads[2][...] = product(left, value_grad[...]).astype(jnp.bfloat16).reshape(shape)
-    summed.turn(1)
     for load in loads:
         load.wait()
 
@@ -1099,12 +1121,11 @@
         panel = rows[cut, width:]
         picks = panel[:, 0:1].astype(jnp.float32) + panel[:, 1:2].astype(jnp.float32)
         cots[cut] = (cots[cut].astype(jnp.float32) * picks).astype(jnp.bfloat16)
-        lanes = pl.ds(pl.multiple_of(replica * share, share), share)
-        rows_left[:, cut] = rows[cut, lanes].T
         return carry
 
     lax.fori_loop(0, total_rows // 256, weigh, 0)
-    turn_tiles = (0, 2, 4, 6, 8, 10)
+    summed.turn(1)
+    turn_tiles = (1, 3, 5, 7, 9, 10)
     blocks = 1 if chunk <= 512 else 2
 
     def each_tile(turn, carry):
@@ -1134,8 +1155,10 @@
             tiles_of[slot, 0, cut] = (value * up_part).astype(jnp.bfloat16)
             tiles_of[slot, 1, cut] = (back * up_part * slope).astype(jnp.bfloat16)
             tiles_of[slot, 2, cut] = (back * value).astype(jnp.bfloat16)
-        for number in range(2):
-            out_tiles[number, slot] = product(rows_left[...], tiles_of[slot, number + 1])
+        both = jnp.concatenate([tiles_of[slot, 1], tiles_of[slot, 2]], axis=1)
+        turned = product_left(both, rows[:, share_lanes]).T
+        out_tiles[0, slot] = turned[:, :tile]
+        out_tiles[1, slot] = turned[:, tile:]
         start_all(out_copies(at, slot))
 
         @pl.when(turn < spans)
@@ -1149,31 +1172,14 @@
     offset = pl.multiple_of(replica * hidden_share - first * tile, 8)
     down_copy = pltpu.make_async_copy(down_tiles.at[pl.ds(offset, hidden_share)], down_out, down_sem)
     down_copy.start()
-    experts, room, capacity = slot_sizes
-    tok = normed.shape[0]
-    live = iota((tok, 1), 0) + lax.axis_index("erow") * tok < lengths[0]
-    slots = column_slots(columns_of(near_row[...], 2), live, experts, room, capacity)
-    names = iota((tok, experts * room), 1).astype(jnp.float32)
-    columns = columns_of(routes_true[...], 2)
-    lane = iota((tok, LANES), 1).astype(jnp.float32)
-    total = residual[...]
-    wait_all(returns)
-    results = out_landed[...].reshape(experts * room, width)
-    for k in range(2):
-        hot = jnp.where(names == slots[k], 1.0, 0.0).astype(jnp.bfloat16)
-        pick = jnp.sum(jnp.where(columns[:, k : k + 1] == lane, gates_in[...], 0.0), axis=1, keepdims=True)
-        total = total + pick * product(hot, results)
-    output[...] = total.astype(jnp.bfloat16)
     for turn in (tiles - 2, tiles - 1):
         wait_all(out_copies(tile_at(turn), turn % 2))
     down_copy.wait()
 
 
-def last(sizes, number, slot_sizes, placing, shared, small, rows_in, cots_in, parts_in, out_sent, weights):
+def last(sizes, number, grads, small, rows_in, cots_in, parts_in, weights):
     n_dp, n_row, n_col = sizes
-    normed = shared[0]
-    tok, width = normed.shape
-    hidden_width = weights[0].shape[1]
+    width, hidden_width = weights[0].shape
     total_rows = sum(piece.shape[0] for piece in rows_in)
     tile = parts_in.shape[3]
     depth = width // (n_dp * n_row * n_col)
@@ -1184,20 +1190,14 @@
     hidden_share = hidden_width // n_dp
     spans = -(-hidden_share // tile) + 1
     scratch = [
-        pltpu.VMEM(out_sent.shape, half),
-        pltpu.SemaphoreType.DMA,
-        pltpu.SemaphoreType.DMA((n_row * n_col - 1,)),
-        pltpu.SemaphoreType.DMA((n_row * n_col - 1,)),
         pltpu.VMEM((total_rows, width + LANES), half),
         pltpu.VMEM((total_rows, width), half),
-        pltpu.VMEM((width // n_dp, total_rows), half),
         pltpu.VMEM((2, 2, width, tile), half),
         pltpu.VMEM((2, 3, total_rows, tile), half),
         pltpu.VMEM((2, tile, width), half),
         pltpu.VMEM((2, 2, width // n_dp, tile), single),
         pltpu.VMEM((spans * tile, width), single),
     ]
-    scratch += [pltpu.VMEM((2, 2, n_row, strip, width), half)] * 3
     for _ in range(3):
         scratch += share_scratch((n_row, n_col), depth, width, half)
     scratch += share_scratch((n_row, n_col), depth, LANES, single)
@@ -1214,17 +1214,17 @@
     out_shape = [jax.ShapeDtypeStruct((depth, width), single)] * 3
     out_shape += [jax.ShapeDtypeStruct((depth, LANES), single)]
     out_shape += [jax.ShapeDtypeStruct((width // n_dp, hidden_width), single)] * 2
-    out_shape += [jax.ShapeDtypeStruct((hidden_share, width), single), jax.ShapeDtypeStruct((tok, width), half)]
+    out_shape += [jax.ShapeDtypeStruct((hidden_share, width), single)]
     return pl.pallas_call(
-        functools.partial(last_kernel, tile, (n_row, n_col), depth, slot_sizes),
+        functools.partial(last_kernel, tile, (n_row, n_col), depth),
         out_shape=out_shape,
-        in_specs=[pl.BlockSpec(memory_space=pltpu.SMEM)] + [vmem] * 9 + [anywhere] * (2 * len(rows_in) + 5),
-        out_specs=[vmem] * 4 + [anywhere] * 3 + [vmem],
+        in_specs=[vmem] * 4 + [anywhere] * (2 * len(rows_in) + 4),
+        out_specs=[vmem] * 4 + [anywhere] * 3,
         scratch_shapes=scratch,
         compiler_params=pltpu.CompilerParams(
             collective_id=number, has_side_effects=True, vmem_limit_bytes=VMEM_LIMIT
         ),
-    )(*placing, *shared, small, *rows_in, *cots_in, parts_in, out_sent, *weights)
+    )(*grads, small, *rows_in, *cots_in, parts_in, *weights)
 
 
 def finish_kernel(experts, bias_share, small, *refs):
@@ -1313,7 +1313,7 @@
     )
     router = router_weight.T
     dims = (head_count, expert_count, room, capacity, n_row, n_col)
-    normed, queries, both, probs, mixed, residual, gates, slot_rows, got_grads, *cots0 = front(
+    normed, queries, both, probs, mixed, residual, gates, slot_rows, got_grads, *cots01 = front(
         dims,
         0,
         lengths,
@@ -1331,12 +1331,12 @@
         out_weight,
     )
     back, got, expert_out, parts, *moved = experts_apply(
-        (n_row, n_col), 1, 256 if slot_count <= 768 else LANES, slot_rows, got_grads, *cots0, gate_mat, up_mat, down_mat
-    )
-    cots1, cots2, cots3, rows0, rows1 = (moved[at : at + 2] for at in range(0, 10, 2))
+        (n_row, n_col), 1, 256 if slot_count <= 768 else LANES, slot_rows, got_grads, *cots01, gate_mat, up_mat, down_mat
+    )
+    cots0, cots1, cots2, cots3, rows0, rows1, rows2 = ((cots01 + moved)[at : at + 2] for at in range(0, 14, 2))
     depth = width // device_count
     bias_share = head_count * bucket_count // device_count
-    token_grad, query_grad, key_grad, value_grad, small, *moved, out_sum = backward(
+    output, token_grad, query_wgrad, key_wgrad, value_wgrad, small, *rows3, out_sum = backward(
         dims + (bias_share, depth),
         2,
         lengths,
@@ -1353,25 +1353,23 @@
         probs,
         queries,
         both,
+        normed,
         back,
+        expert_out,
         got,
         query_weight,
         key_weight,
         value_weight,
         out_weight,
     )
-    rows2, rows3 = moved[:2], moved[2:]
-    query_sum, key_sum, value_sum, small_sum, gate_total, up_total, down_total, output = last(
+    query_sum, key_sum, value_sum, small_sum, gate_total, up_total, down_total = last(
         (n_dp, n_row, n_col),
         3,
-        (expert_count, room, capacity),
-        (lengths, near_routes, routes_row, residual, gates),
-        (normed, query_grad, key_grad, value_grad),
+        (query_wgrad, key_wgrad, value_wgrad),
         small,
         paired(got, rows0, rows1, rows2, rows3),
         paired(got_grads, cots0, cots1, cots2, cots3),
         parts,
-        expert_out,
         (gate_mat, up_mat, down_mat),
     )
     handed = finish(

time: 254 us -> 238 us (0.937)
  Pallas kernels: 251 us -> 235 us
    pallas_call x1, Pallas kernels: 91.1 us -> 82.1 us  [experts_apply(): pl.pallas_call(functools.partial(expert_kernel, tile, sizes), out_shape=[...]
    pallas_call x1, Pallas kernels: 67.3 us -> 59.2 us  [last(): pl.pallas_call(functools.partial(last_kernel, tile, (n_row, n_col), depth...]
    pallas_call x1, Pallas kernels: 34.2 us -> 39.8 us  [front(): pl.pallas_call(functools.partial(front_kernel, dims), out_shape=[jax.Shap...]
    pallas_call x1, Pallas kernels: 48.7 us -> 44.7 us  [backward(): pl.pallas_call(functools.partial(back_kernel, dims), out_shape=[jax.Shape...]
where the time goes in v2:
time: 238 us
  Pallas kernels  235 us (99%)
    pallas_call x1, Pallas kernels, experts_apply(): pl.pallas_call(functools.partial(expert_kernel, tile, sizes), out_shape=[...  82.1 us
    pallas_call x1, Pallas kernels, last(): pl.pallas_call(functools.partial(last_kernel, tile, (n_row, n_col), depth...  59.2 us
    pallas_call x1, Pallas kernels, backward(): pl.pallas_call(functools.partial(back_kernel, dims), out_shape=[jax.Shape...  44.7 us
    pallas_call x1, Pallas kernels, front(): pl.pallas_call(functools.partial(front_kernel, dims), out_shape=[jax.Shap...  39.8 us
    pallas_call x1, Pallas kernels, finish(): pl.pallas_call(functools.partial(finish_kernel, experts, bias_share), out...  9.62 us

profile of v2, /device:TPU:0, one launch (start us, length us, event | category | flops | bytes accessed | tf_op | source)
XLA Modules:
  0.0 238.2 jit_solution(506912234355862929)
XLA Ops:
  1.3 1.3 xor_add_fusion.routes_row.near_row
  2.6 39.8 %shard_map.246 = (bf16[256,1024]{1,0:T(8,128)(2,1)}, bf16[256,1024]{1,0:T(8,128)(2,1)}, bf16[512,2048]{1,0:T(8,128)(2,1)}, bf16[16,256,512]{2,1,0:T(8,128)(2,1)}...) custom-call(s32[1]{0:T(128)S(6)} %copy.28.lengths, ...), custom_call_target="tpu_custom_call" | custom-call | tf_op jit(solution)/shard_map/pallas_call | solution.py:448
  42.4 82.1 %shard_map.247 = (bf16[8,80,1152]{2,1,0:T(8,128)(2,1)}, bf16[8,80,1152]{2,1,0:T(8,128)(2,1)}, bf16[8,80,1024]{2,1,0:T(8,128)(2,1)}, bf16[11,3,1600,256]{3,2,1,0:...) custom-call(bf16[8,80,1152]{2,1,0:T(8,128)(2,1)} %get-tuple-element., ...), custom_call_target="tpu_custom_call" | custom-call | tf_op jit(solution)/shard_map/pallas_call | solution.py:718
  124.5 44.7 %shard_map.248 = (bf16[256,1024]{1,0:T(8,128)(2,1)}, f32[256,1024]{1,0:T(8,128)}, bf16[2,2,2,128,1024]{4,3,2,1,0:T(8,128)(2,1)}, bf16[2,2,2,128,1024]{4,3,2,1,0:...) custom-call(s32[1]{0:T(128)S(6)} %copy.28.lengths, ...), custom_call_target="tpu_custom_call" | custom-call | tf_op jit(solution)/shard_map/pallas_call | solution.py:1021
  169.2 59.2 %shard_map.249 = (f32[32,1024]{1,0:T(8,128)}, f32[32,1024]{1,0:T(8,128)}, f32[32,1024]{1,0:T(8,128)}, f32[32,128]{1,0:T(8,128)}, f32[256,2816]{1,0:T(8,128)}, /*index=5*/f32[256,2816]{1,0:T(8,128)}, f32[704,1024]{1,0:T(8,128)}) custom-call(bf16[2,2,2,128,1024]{4,3,2,1,0:T(8,128)(2,1)} %get-tuple-element.84.refs_0_, ...), custom_call_target="tpu_custom_call" | custom-call | tf_op jit(solution)/shard_map/pallas_call | solution.py:1218
  228.4 9.6 %shard_map.250 = (bf16[256,1024]{1,0:T(8,128)(2,1)}, f32[256,1024]{1,0:T(8,128)}, f32[32,1024]{1,0:T(8,128)}, f32[32,1024]{1,0:T(8,128)}, f32[32,1024]{1,0:T(8,1...) custom-call(f32[32,128]{1,0:T(8,128)} %get-tuple-element.102.small, ...), custom_call_target="tpu_custom_call" | custom-call | tf_op jit(solution)/shard_map/pallas_call | solution.py:1257

commit v3 on v2

--- a/solution.py
+++ b/solution.py
@@ -1054,11 +1054,12 @@
 
 def last_kernel(tile, sizes, depth, *refs):
     pieces = 9
-    grads, small, refs = refs[:3], refs[3], refs[4:]
+    grads_in, small, refs = refs[:3], refs[3], refs[4:]
     rows_in, refs = refs[:pieces], refs[pieces:]
     cots_in, refs = refs[:pieces], refs[pieces:]
     parts_in, weights, sums, refs = refs[0], refs[1:4], refs[4:8], refs[8:]
     (gate_out, up_out, down_out), refs = refs[:3], refs[3:]
+    grads, grad_sems, refs = refs[:3], refs[3], refs[4:]
     (rows, cots, mats, tiles_of, own_mats, out_tiles, down_tiles), refs = refs[:7], refs[7:]
     held, refs = [refs[5 * at : 5 * at + 5] for at in range(4)], refs[20:]
     load_sems, weight_sems, own_sems, out_sems, down_sem, send_sems, recv_sems = refs
@@ -1075,6 +1076,11 @@
     barrier = pltpu.get_barrier_semaphore()
     for device in summed.devices:
         pl.semaphore_signal(barrier, 1, device_id=device, device_id_type=MESH)
+    grad_loads = [
+        pltpu.make_async_copy(source, target, grad_sems.at[at])
+        for at, (source, target) in enumerate(zip(grads_in, grads))
+    ]
+    start_all(grad_loads)
     loads, start = [], 0
     for at, (row_piece, cot_piece) in enumerate(zip(rows_in, cots_in)):
         size = row_piece.shape[0]
@@ -1111,6 +1117,7 @@
         return lax.rem(first + turn, tiles)
 
     start_all(weight_loads(tile_at(0), 0) + own_loads(tile_at(0), 0))
+    wait_all(grad_loads)
     pl.semaphore_wait(barrier, len(summed.devices))
     summed.turn(0)
     for load in loads:
@@ -1189,7 +1196,8 @@
     small = small.reshape(2, 2, n_row, strip, small.shape[1])
     hidden_share = hidden_width // n_dp
     spans = -(-hidden_share // tile) + 1
-    scratch = [
+    scratch = [pltpu.VMEM(grad.shape, half) for grad in grads] + [pltpu.SemaphoreType.DMA((3,))]
+    scratch += [
         pltpu.VMEM((total_rows, width + LANES), half),
         pltpu.VMEM((total_rows, width), half),
         pltpu.VMEM((2, 2, width, tile), half),
@@ -1218,7 +1226,7 @@
     return pl.pallas_call(
         functools.partial(last_kernel, tile, (n_row, n_col), depth),
         out_shape=out_shape,
-        in_specs=[vmem] * 4 + [anywhere] * (2 * len(rows_in) + 4),
+        in_specs=[anywhere] * 3 + [vmem] + [anywhere] * (2 * len(rows_in) + 4),
         out_specs=[vmem] * 4 + [anywhere] * 3,
         scratch_shapes=scratch,
         compiler_params=pltpu.CompilerParams(

time: 238 us -> 242 us (1.017)
  Pallas kernels: 235 us -> 239 us
    pallas_call x1, Pallas kernels: 59.2 us -> 62.4 us  [last(): pl.pallas_call(functools.partial(last_kernel, tile, (n_row, n_col), depth...]
where the time goes in v3:
time: 242 us; the launch traced here: 241 us
  Pallas kernels  239 us (99%)
    pallas_call x1, Pallas kernels, experts_apply(): pl.pallas_call(functools.partial(expert_kernel, tile, sizes), out_shape=[...  82.1 us
    pallas_call x1, Pallas kernels, last(): pl.pallas_call(functools.partial(last_kernel, tile, (n_row, n_col), depth...  62.4 us
    pallas_call x1, Pallas kernels, backward(): pl.pallas_call(functools.partial(back_kernel, dims), out_shape=[jax.Shape...  44.7 us
    pallas_call x1, Pallas kernels, front(): pl.pallas_call(functools.partial(front_kernel, dims), out_shape=[jax.Shap...  39.8 us
    pallas_call x1, Pallas kernels, finish(): pl.pallas_call(functools.partial(finish_kernel, experts, bias_share), out...  9.62 us

profile of v3, /device:TPU:0, one launch (start us, length us, event | category | flops | bytes accessed | tf_op | source)
XLA Modules:
  0.0 241.4 jit_solution(11589830151484186262)
XLA Ops:
  1.3 1.3 xor_add_fusion.routes_row.near_row
  2.6 39.8 %shard_map.246 = (bf16[256,1024]{1,0:T(8,128)(2,1)}, bf16[256,1024]{1,0:T(8,128)(2,1)}, bf16[512,2048]{1,0:T(8,128)(2,1)}, bf16[16,256,512]{2,1,0:T(8,128)(2,1)}...) custom-call(s32[1]{0:T(128)S(6)} %copy.28.lengths, ...), custom_call_target="tpu_custom_call" | custom-call | tf_op jit(solution)/shard_map/pallas_call | solution.py:448
  42.4 82.1 %shard_map.247 = (bf16[8,80,1152]{2,1,0:T(8,128)(2,1)}, bf16[8,80,1152]{2,1,0:T(8,128)(2,1)}, bf16[8,80,1024]{2,1,0:T(8,128)(2,1)}, bf16[11,3,1600,256]{3,2,1,0:...) custom-call(bf16[8,80,1152]{2,1,0:T(8,128)(2,1)} %get-tuple-element., ...), custom_call_target="tpu_custom_call" | custom-call | tf_op jit(solution)/shard_map/pallas_call | solution.py:718
  124.5 44.7 %shard_map.248 = (bf16[256,1024]{1,0:T(8,128)(2,1)}, f32[256,1024]{1,0:T(8,128)}, bf16[2,2,2,128,1024]{4,3,2,1,0:T(8,128)(2,1)}, bf16[2,2,2,128,1024]{4,3,2,1,0:...) custom-call(s32[1]{0:T(128)S(6)} %copy.28.lengths, ...), custom_call_target="tpu_custom_call" | custom-call | tf_op jit(solution)/shard_map/pallas_call | solution.py:1021
  169.2 62.4 %shard_map.249 = (f32[32,1024]{1,0:T(8,128)}, f32[32,1024]{1,0:T(8,128)}, f32[32,1024]{1,0:T(8,128)}, f32[32,128]{1,0:T(8,128)}, f32[256,2816]{1,0:T(8,128)}, /*index=5*/f32[256,2816]{1,0:T(8,128)}, f32[704,1024]{1,0:T(8,128)}) custom-call(bf16[2,2,2,128,1024]{4,3,2,1,0:T(8,128)(2,1)} %get-tuple-element.84.refs_0_, ...), custom_call_target="tpu_custom_call" | custom-call | tf_op jit(solution)/shard_map/pallas_call | solution.py:1226
  231.6 9.6 %shard_map.250 = (bf16[256,1024]{1,0:T(8,128)(2,1)}, f32[256,1024]{1,0:T(8,128)}, f32[32,1024]{1,0:T(8,128)}, f32[32,1024]{1,0:T(8,128)}, f32[32,1024]{1,0:T(8,1...) custom-call(f32[32,128]{1,0:T(8,128)} %get-tuple-element.102.small, ...), custom_call_target="tpu_custom_call" | custom-call | tf_op jit(solution)/shard_map/pallas_call | solution.py:1265
